TPU v7x, 256 devices: a whole 4x4x8 slice. The times are simulated.
256 devices in a mesh: dp: 4 (over y), expert: 64 (over x, z, core).
Axes of the slice: x: 4, y: 4, z: 8, core: 2. Of those that a mesh axis runs over, the one named last changes fastest.
Arguments:
- grad_out: bfloat16 [32768, 2048], P(('dp', 'expert')), may hold values from -6 to 6
- layer_input: bfloat16 [32768, 2048], P(('dp', 'expert')), may hold values from -0.8984375 to 0.8984375
- router_weight: bfloat16 [2048, 128], replicated, may hold values from -6 to 6
- gate_probs: float32 [32768, 8], P(('dp', 'expert')), may hold values from 0 to 1, as said below
- expert_ids: int32 [32768, 8], P(('dp', 'expert')), may hold values from 0 to 127, all different within a row; in each aligned block of 128 rows (0 to 127, 128 to 255, ...) at most 9 rows name the same one
- expert_out: bfloat16 [4, 128, 64, 9, 2048], P('dp', 'expert'), may hold values from -0.1875 to 0.1875
Outputs:
- grad_expert_out: bfloat16 [4, 128, 64, 9, 2048], P('dp', 'expert')
- grad_input: bfloat16 [32768, 2048], P(('dp', 'expert'))
- grad_router: float32 [2048, 128], replicated
Inputs may be any that keep to these rules, and one draw needn't show every extreme that they name: `expert_ids`: each token names 8 different experts; among the 128 tokens of one device no expert is named more than 9 times, a bound that some block reaches. `gate_probs`: each row is positive and sums to one.
All inputs are finite; a program needn't handle non-finite values.
Results may differ from a plain program's by a relative error of at most 0.012.
Values may be sent and summed in bfloat16 or wider, within the bound.
A program may use at most 128 MiB of HBM per device.

v0:
```python
import jax
import jax.numpy as jnp
from jax import lax
from jax.sharding import PartitionSpec as P


def slot_table(ids, count):
    flat = ids.reshape(-1)
    onehot = (flat[:, None] == jnp.arange(count, dtype=jnp.int32)[None, :]).astype(jnp.int32)
    before = jnp.cumsum(onehot, axis=0) - onehot
    return jnp.sum(before * onehot, axis=1).reshape(ids.shape)


def body(grad_out, layer_input, router_weight, gate_probs, expert_ids, expert_out):
    tokens, width = grad_out.shape
    top = expert_ids.shape[1]
    total = router_weight.shape[1]
    devices = lax.axis_size("expert")
    local = total // devices
    slots = expert_out.shape[3]
    slot = slot_table(expert_ids, total)
    owner = expert_ids // local
    which = expert_ids % local
    spread = jnp.broadcast_to(grad_out[:, None, :], (tokens, top, width))
    send_rows = (
        jnp.zeros((local, devices, slots, width), jnp.bfloat16).at[which, owner, slot].set(spread)
    )
    send_gates = (
        jnp.zeros((local, devices, slots), jnp.float32).at[which, owner, slot].set(gate_probs)
    )
    rows, gates = (
        lax.all_to_all(send_rows, "expert", split_axis=1, concat_axis=1, tiled=True),
        lax.all_to_all(
            send_gates.astype(jnp.bfloat16), "expert", split_axis=1, concat_axis=1, tiled=True
        ).astype(send_gates.dtype),
    )
    mine = expert_out[0]
    grad_y = (gates[..., None] * rows.astype(jnp.float32)).astype(jnp.bfloat16)
    scores = jnp.einsum("lncd,lncd->lnc", rows, mine, preferred_element_type=jnp.float32)
    returned = lax.all_to_all(scores, "expert", split_axis=1, concat_axis=1, tiled=True)
    grad_gate = returned[which, owner, slot]
    mean_term = jnp.sum(gate_probs * grad_gate, axis=1, keepdims=True)
    grad_score = gate_probs * (grad_gate - mean_term)
    onehot = (expert_ids[:, :, None] == jnp.arange(total, dtype=jnp.int32)[None, None, :]).astype(
        jnp.float32
    )
    grad_logits = jnp.sum(onehot * grad_score[:, :, None], axis=1).astype(jnp.bfloat16)
    grad_input = lax.dot_general(
        grad_logits, router_weight, (((1,), (1,)), ((), ())), preferred_element_type=jnp.float32
    ).astype(jnp.bfloat16)
    weight_part = lax.dot_general(
        layer_input, grad_logits, (((0,), (0,)), ((), ())), preferred_element_type=jnp.float32
    )
    grad_router = lax.psum(weight_part, ("dp", "expert"))
    return (grad_y[None], grad_input, grad_router)


def solution(mesh):
    return jax.shard_map(
        body,
        mesh=mesh,
        in_specs=(
            P(("dp", "expert"), None),
            P(("dp", "expert"), None),
            P(),
            P(("dp", "expert"), None),
            P(("dp", "expert"), None),
            P("dp", "expert", None, None, None),
        ),
        out_specs=(P("dp", "expert", None, None, None), P(("dp", "expert"), None), P()),
        check_vma=False,
    )
```

profile of v0, /device:TPU:1, one launch (start us, length us, event | category | flops | bytes accessed | tf_op | source)
XLA Modules:
  0.0 461.2 jit_solution(9650145365506725132)
XLA Ops:
  7.2 0.8 copy.104
  8.2 0.7 fusion.12
  9.9 0.7 shift-left_or_fusion
  10.6 0.7 and_reduce_fusion
  11.4 0.7 multiply_reduce_fusion.2
  12.3 9.4 %scatter_custom_fusion.1 = bf16[1152,2048]{1,0:T(8,128)(2,1)} fusion(s32[1024]{0:T(1024)S(1)} %reshape.82, bf16[]{:T(256)} %constant.42.clone.1, bf16[128,2048]{1,0:T(8,128)(2,1)S(1)} %copy-done), kind=kCustom, calls=%fused_computation.6 | custom fusion | bytes 5242882
  21.7 9.4 %copy.117 = bf16[2,64,9,2048]{3,0,2,1:T(2,128)(2,1)} copy(bf16[2,64,9,2048]{3,1,2,0:T(8,128)(2,1)} %bitcast.37) | data formatting | bytes 9437184 | tf_op jit(solution)/shard_map/scatter | solution.py:26
  31.1 13.5 %all-to-all-start.1 = ((bf16[2,64,9,2048]{3,0,2,1:T(2,128)(2,1)}), bf16[2,64,9,2048]{3,0,2,1:T(2,128)(2,1)}, u32[]{:S(2)}, u32[]{:S(2)}) async-start(bf16[2,64,9,2048]{3,0,2,1:T(2,128)(2,1)} %copy.117), calls=%async_computation.1 | async-start | bytes 9437184 | tf_op jit(solution)/shard_map/all_to_all | solution.py:32
  45.0 4.3 scatter_custom_fusion
  49.4 0.7 copy.113
  50.1 101.6 %all-to-all-done.1 = bf16[2,64,9,2048]{3,0,2,1:T(2,128)(2,1)} async-done(((bf16[2,64,9,2048]{3,0,2,1:T(2,128)(2,1)}), bf16[2,64,9,2048]{3,0,2,1:T(2,128)(2,1)}, u32[]{:S(2)}, u32[]{:S(2)}) %all-to-all-start.1) | async-done | bytes 4718624 | tf_op jit(solution)/shard_map/all_to_all | solution.py:32
  151.7 5.8 %all-to-all-start = ((bf16[2,64,9]{2,0,1:T(2,128)(2,1)}), bf16[2,64,9]{2,0,1:T(2,128)(2,1)S(1)}, u32[]{:S(2)}, u32[]{:S(2)}) async-start(bf16[2,64,9]{2,0,1:T(2,128)(2,1)} %copy.113), calls=%async_computation | async-start | bytes 65536 | tf_op jit(solution)/shard_map/all_to_all | solution.py:33
  157.6 6.7 %convert_element_type.30 = f32[2,64,9,2048]{3,0,2,1:T(2,128)S(1)} convert(bf16[2,64,9,2048]{3,0,2,1:T(2,128)(2,1)} %all-to-all-done.1) | non-fusion elementwise | flops 2359296 | bytes 14155776 | tf_op jit(solution)/shard_map/convert_element_type | solution.py:38
  164.3 5.3 %multiply_reduce_fusion = f32[2,64,9]{1,2,0:T(8,128)S(1)} fusion(f32[2,64,9,2048]{3,0,2,1:T(2,128)S(1)} %convert_element_type.30, bf16[1,2,64,9,2048]{4,2,3,1,0:T(8,128)(2,1)S(1)} %bitcast.39), kind=kLoop, calls=%fused_computation.3 | loop fusion | flops 7076736 | bytes 14160384
  169.6 0.7 copy.128
  170.4 10.3 %all-to-all-start.2 = ((f32[2,64,9]{2,0,1:T(2,128)}), f32[2,64,9]{2,0,1:T(2,128)S(1)}, u32[]{:S(2)}, u32[]{:S(2)}) async-start(f32[2,64,9]{2,0,1:T(2,128)} %copy.128), calls=%async_computation.2 | async-start | bytes 131072 | tf_op jit(solution)/shard_map/all_to_all | solution.py:40
  181.6 8.9 %all-to-all-done.2 = f32[2,64,9]{2,0,1:T(2,128)S(1)} async-done(((f32[2,64,9]{2,0,1:T(2,128)}), f32[2,64,9]{2,0,1:T(2,128)S(1)}, u32[]{:S(2)}, u32[]{:S(2)}) %all-to-all-start.2) | async-done | bytes 4640 | tf_op jit(solution)/shard_map/all_to_all | solution.py:40
  190.5 9.8 %gather_fusion = f32[1024]{0:T(1024)S(1)} fusion(f32[2,64,9]{2,0,1:T(2,128)S(1)} %all-to-all-done.2, s32[1024]{0:T(1024)S(1)} %reshape.70), kind=kCustom, calls=%fused_computation | custom fusion | bytes 20480 | tf_op jit(solution)/shard_map/gather | solution.py:41
  200.9 1.3 convolution_bitcast_fusion
  202.3 8.2 %fusion = bf16[1,2,64,9,2048]{4,1,3,2,0:T(2,128)(2,1)} fusion(f32[2,64,9]{0,2,1:T(8,128)S(1)} %copy.115, bf16[2,64,9,2048]{3,0,2,1:T(2,128)(2,1)} %all-to-all-done.1), kind=kLoop, calls=%fused_computation.5 | loop fusion | flops 7077888 | bytes 9441792 | tf_op jit(solution)/shard_map/broadcast_in_dim | solution.py:55
  210.5 6.7 %copy.122 = bf16[1,2,64,9,2048]{4,2,3,1,0:T(8,128)(2,1)} copy(bf16[1,2,64,9,2048]{4,1,3,2,0:T(2,128)(2,1)} %fusion) | data formatting | bytes 9437184
  217.2 1.1 convolution_convert_fusion
  218.3 233.4 %all-reduce.2.cloned.1.call-done = f32[2048,128]{0,1:T(8,128)} async-done(((f32[2048,128]{0,1:T(8,128)}), f32[2048,128]{0,1:T(8,128)}) %all-reduce.2.cloned.1.call-update) | async-done | bytes 1048592 | tf_op jit(solution)/shard_map/psum | solution.py:54
  451.8 2.5 copy.123
  (45 shorter events, 3.4 us)
Async XLA Ops:
  7.2 5.2 %copy-start = (bf16[128,2048]{1,0:T(8,128)(2,1)S(1)}, bf16[128,2048]{1,0:T(8,128)(2,1)}, u32[]{:S(2)}) copy-start(bf16[128,2048]{1,0:T(8,128)(2,1)} %param.6) | copy-start | bytes 1572868
  31.1 13.5 %copy-start.3 = (f32[128,8]{0,1:T(8,128)S(1)}, f32[128,8]{0,1:T(8,128)}, u32[]{:S(2)}) copy-start(f32[128,8]{0,1:T(8,128)} %param.9) | copy-start | bytes 12292
  31.1 133.2 %slice-start = ((s8[4718592]{0:T(1024)(128)(4,1)}), s8[524288]{0:T(1024)(128)(4,1)S(1)}, s32[]{:S(2)}) async-start(s8[4718592]{0:T(1024)(128)(4,1)} %bitcast.38), calls=%async_computation.4 | async-start | bytes 1048576
  31.1 120.6 %all-to-all-start.1 = ((bf16[2,64,9,2048]{3,0,2,1:T(2,128)(2,1)}), bf16[2,64,9,2048]{3,0,2,1:T(2,128)(2,1)}, u32[]{:S(2)}, u32[]{:S(2)}) async-start(bf16[2,64,9,2048]{3,0,2,1:T(2,128)(2,1)} %copy.117), calls=%async_computation.1 | async-start | bytes 9437184 | tf_op jit(solution)/shard_map/all_to_all | solution.py:32
  151.7 18.7 %all-to-all-start = ((bf16[2,64,9]{2,0,1:T(2,128)(2,1)}), bf16[2,64,9]{2,0,1:T(2,128)(2,1)S(1)}, u32[]{:S(2)}, u32[]{:S(2)}) async-start(bf16[2,64,9]{2,0,1:T(2,128)(2,1)} %copy.113), calls=%async_computation | async-start | bytes 65536 | tf_op jit(solution)/shard_map/all_to_all | solution.py:33
  157.6 6.7 %slice-start.1 = ((s8[4718592]{0:T(1024)(128)(4,1)}), s8[4194304]{0:T(1024)(128)(4,1)S(1)}, s32[]{:S(2)}) async-start(s8[4718592]{0:T(1024)(128)(4,1)} %bitcast.38), calls=%async_computation.5 | async-start | bytes 8388608
  170.4 20.1 %all-to-all-start.2 = ((f32[2,64,9]{2,0,1:T(2,128)}), f32[2,64,9]{2,0,1:T(2,128)S(1)}, u32[]{:S(2)}, u32[]{:S(2)}) async-start(f32[2,64,9]{2,0,1:T(2,128)} %copy.128), calls=%async_computation.2 | async-start | bytes 131072 | tf_op jit(solution)/shard_map/all_to_all | solution.py:40
  180.7 271.1 %all-reduce.2.cloned.1.call-start = ((), (), s32[]{:S(2)}) async-start(), calls=%async_computation.3 | async-start | bytes 2097152 | tf_op jit(solution)/shard_map/psum | solution.py:54
  181.6 19.4 %copy-start.1 = (bf16[128,2048]{1,0:T(8,128)(2,1)S(1)}, bf16[128,2048]{1,0:T(8,128)(2,1)}, u32[]{:S(2)}) copy-start(bf16[128,2048]{1,0:T(8,128)(2,1)} %param.7) | copy-start | bytes 1572868
  210.5 6.7 %copy-start.2 = (bf16[2048,128]{1,0:T(8,128)(2,1)S(1)}, bf16[2048,128]{1,0:T(8,128)(2,1)}, u32[]{:S(2)}) copy-start(bf16[2048,128]{1,0:T(8,128)(2,1)} %param.8) | copy-start | bytes 1572868
Sparse Core Ops, SparseCore 0:
  202.4 249.3 all-reduce.1
where the time goes:
time: 462 us; the launch traced here: 461 us
  waiting for transfers between devices  344 us (74%)
  local copies, waits for them, and re-layouts  46.3 us (10%)
  starting transfers between devices  29.9 us (6%)
  other arithmetic  24.4 us (5%)
  between operations  14.2 us (3%)
    psum x1, waiting for transfers between devices, body(): grad_router = lax.psum(weight_part, ('dp', 'expert'))  233 us
    all_to_all x1, waiting for transfers between devices, body(): lax.all_to_all(send_rows, 'expert', split_axis=1, concat_axis=1, tiled=True)  102 us
    unnamed x23, local copies, waits for them, and re-layouts  24.4 us
    all_to_all x1, starting transfers between devices, body(): lax.all_to_all(send_rows, 'expert', split_axis=1, concat_axis=1, tiled=True)  13.5 us
    all_to_all x1, starting transfers between devices, body(): lax.all_to_all(scores, 'expert', split_axis=1, concat_axis=1, tiled=True)  10.3 us
    gather x2, local copies, waits for them, and re-layouts, body(): grad_gate = returned[which, owner, slot]  9.85 us
    scatter x1, local copies, waits for them, and re-layouts, body(): jnp.zeros((local, devices, slots, width), jnp.bfloat16)  9.36 us
  transfers between devices with their start and end apart: 4, of which 3 were waited for; matrix products, arithmetic and copies ran while one was open for 8% of the time, Pallas kernels for 0%

commit v1 on v0

v1 whole, which is shorter than its diff:
```python
import jax
import jax.numpy as jnp
from jax import lax
from jax.experimental import pallas as pl
from jax.experimental.pallas import tpu as pltpu
from jax.sharding import PartitionSpec as P

MESH = pl.DeviceIdType.MESH
BF, F32 = jnp.bfloat16, jnp.float32
NX, NZ, NY = 4, 8, 4
D, TOK, TOP, EXP, CAP = 2048, 128, 8, 128, 9
ROWS = 2 * CAP
PAIRS, SUBS, WID = 4, 2, 256
HOPS = ((4, 3), (3, 4))
REL = ((2, 0), (2, 1), (1, 0), (3, 0), (1, 1), (3, 1), (0, 1), (0, 0))


def iota(shape, axis):
    return lax.broadcasted_iota(jnp.int32, shape, axis)


def dot(a, b, dims=((1,), (0,))):
    return lax.dot_general(a, b, (dims, ((), ())), preferred_element_type=F32)


def earlier():
    return (iota((TOK, TOK), 0) < iota((TOK, TOK), 1)).astype(BF)


def kernel(
    go, li, rw, meta, eo, grows, gin, grout,
    x_buf, o_buf, w_buf, r_buf, e_buf, mb, slots, gates, m_buf, mask,
    own_slot, own_gate, acc, s_out, t_in, lib, lit, glt, glb, part, rb, fin, ag, half, agb,
    loc, xch_s, xch_r, ring_s, ring_r, meta_s, meta_r, li_s, li_r, x_s, x_r,
    sc_s, sc_r, gl_s, gl_r, rs_s, rs_r, a1_s, a1_r, a2_s, a2_r, a3_s, a3_r,
):
    y = lax.axis_index("dp")
    idx = lax.axis_index("expert")
    x, z, c = idx // 16, (idx // 2) % NZ, idx % 2

    def at(dx=0, dy=0, dz=0, dc=0):
        xx, zz, cc = lax.rem(x + dx, NX), lax.rem(z + dz, NZ), lax.rem(c + dc, 2)
        return (lax.rem(y + dy, NY), xx * 16 + zz * 2 + cc)

    def send(src, dst, ss, rs, to):
        return pltpu.make_async_remote_copy(
            src_ref=src, dst_ref=dst, send_sem=ss, recv_sem=rs, device_id=to, device_id_type=MESH
        )

    load_e = pltpu.make_async_copy(eo, e_buf, loc.at[0])
    load_e.start()
    own_half = []
    for p in range(PAIRS):
        cols = pl.ds(pl.multiple_of(c * 1024 + p * WID, WID), WID)
        cp = pltpu.make_async_copy(
            go.at[:, cols], x_buf.at[p, pl.ds((2 * z + c) * TOK, TOK)], loc.at[1 + p]
        )
        cp.start()
        own_half.append(cp)
    own_li = pltpu.make_async_copy(
        li.at[:, pl.ds(pl.multiple_of((2 * y + c) * WID, WID), WID)], lib.at[2 * y + c], loc.at[5]
    )
    own_li.start()
    own_meta = pltpu.make_async_copy(meta, mb.at[pl.ds((2 * z + c) * 16, 16)], loc.at[6])
    own_meta.start()

    barrier = pltpu.get_barrier_semaphore()
    zc = [(dz, dc) for dz in range(NZ) for dc in range(2) if dz or dc]
    yc = [(dy, dc) for dy in range(NY) for dc in range(2) if dy or dc]
    greet = [dict(dz=a, dc=b) for a, b in zc]
    greet += [dict(dx=a, dc=b) for a, b in REL if a]
    greet += [dict(dy=a, dc=b) for a, b in yc if a]
    for g in greet:
        pl.semaphore_signal(barrier, inc=1, device_id=at(**g), device_id_type=MESH)
    pl.semaphore_wait(barrier, len(greet))

    pending = []

    swap = []
    for p in range(PAIRS):
        cols = pl.ds(pl.multiple_of((1 - c) * 1024 + p * WID, WID), WID)
        cp = send(
            go.at[:, cols], x_buf.at[p, pl.ds((2 * z + c) * TOK, TOK)],
            xch_s.at[p], xch_r.at[p], at(dc=1),
        )
        cp.start()
        swap.append(cp)

    meta_cp = []
    for i, (dz, dc) in enumerate(zc):
        cp = send(
            meta, mb.at[pl.ds((2 * z + c) * 16, 16)], meta_s.at[i], meta_r.at[i], at(dz=dz, dc=dc)
        )
        cp.start()
        meta_cp.append(cp)

    def ring(p, s, d, h):
        far = h - 1
        zb = lax.rem(z + (NZ - far if d == 0 else far), NZ)
        blk = x_buf.at[p, pl.ds(zb * 2 * TOK, 2 * TOK), pl.ds(s * 128, 128)]
        return send(
            blk, blk, ring_s.at[p, s, d, h - 1], ring_r.at[p, s, d, h - 1],
            at(dz=1 if d == 0 else NZ - 1),
        )

    def landed(p, s, d, h):
        zb = lax.rem(z + (NZ - h if d == 0 else h), NZ)
        blk = x_buf.at[p, pl.ds(zb * 2 * TOK, 2 * TOK), pl.ds(s * 128, 128)]
        send(
            blk, blk, ring_s.at[p, s, d, h - 1], ring_r.at[p, s, d, h - 1],
            at(dz=1 if d == 0 else NZ - 1),
        ).wait_recv()

    def first(p):
        own_half[p].wait()
        swap[p].wait_recv()
        for s in range(SUBS):
            for d in range(2):
                cp = ring(p, s, d, 1)
                cp.start()
                pending.append(cp)

    def forward(p, s, h):
        for d in range(2):
            if h <= HOPS[s][d]:
                landed(p, s, d, h - 1)
                cp = ring(p, s, d, h)
                cp.start()
                pending.append(cp)

    def finish(p):
        for s in range(SUBS):
            for d in range(2):
                landed(p, s, d, HOPS[s][d])

    first(0)

    li_cp = []
    for i, (dy, dc) in enumerate(yc):
        g = 2 * lax.rem(y + dy, NY) + lax.rem(c + dc, 2)
        cp = send(
            li.at[:, pl.ds(pl.multiple_of(g * WID, WID), WID)], lib.at[2 * y + c],
            li_s.at[i], li_r.at[i], at(dy=dy, dc=dc),
        )
        cp.start()
        li_cp.append(cp)

    lane_row = iota((TOK, TOK), 0)
    expert = 2 * lax.rem(lane_row, 64) + lane_row // 64
    named = jnp.zeros((EXP, TOK), F32)
    gate = jnp.zeros((EXP, TOK), F32)
    for k in range(TOP):
        hit = meta[k : k + 1, :].astype(jnp.int32) == expert
        named = jnp.where(hit, 1.0, named)
        gate = jnp.where(hit, meta[8 + k : 9 + k, :], gate)
    before = dot(named.astype(BF), earlier())
    own_slot[...] = jnp.where(named > 0, before, 99.0)
    own_gate[...] = gate
    for b in range(16):
        mask[:, b * TOK : (b + 1) * TOK] = (iota((16, TOK), 0) == b).astype(BF)

    forward(0, 0, 2)
    forward(0, 1, 2)

    own_meta.wait()
    for cp in meta_cp:
        cp.wait_recv()
    ids = [mb[pl.ds(k, 16, stride=16), :].astype(jnp.int32) for k in range(TOP)]
    gts = [mb[pl.ds(8 + k, 16, stride=16), :] for k in range(TOP)]
    for ei in range(16):
        d, l = ei // 2, ei % 2
        e = (d // 2) * 32 + z * 4 + (d % 2) * 2 + l
        nm = jnp.zeros((16, TOK), F32)
        gt = jnp.zeros((16, TOK), F32)
        for k in range(TOP):
            hit = ids[k] == e
            nm = jnp.where(hit, 1.0, nm)
            gt = jnp.where(hit, gts[k], gt)
        m_buf[ei * 16 : (ei + 1) * 16, :] = nm
        gates[ei * 16 : (ei + 1) * 16, :] = gt
    bef = dot(m_buf[...].astype(BF), earlier())
    slots[...] = jnp.where(m_buf[...] > 0, bef, 99.0)

    def build(lo, hi):
        def one(ei, carry):
            base = pl.multiple_of(ei * 16, 16)
            sl = slots[pl.ds(base, 16), :]
            gt = gates[pl.ds(base, 16), :]
            for s in range(CAP):
                w = jnp.where(sl == float(s), gt, 0.0).astype(BF)
                row = pl.multiple_of(ei * (CAP * 16) + s * 16, 16)
                w_buf[pl.ds(row, 16), :] = jnp.concatenate([w] * 16, axis=1) * mask[...]
            return carry

        lax.fori_loop(lo, hi, one, 0)

    forward(0, 0, 3)
    forward(0, 1, 3)
    build(0, 8)
    first(1)
    forward(0, 0, 4)
    forward(0, 1, 4)
    build(8, 16)
    finish(0)

    def place(p, xs, cs):
        cols = pl.ds(pl.multiple_of(cs * 1024 + p * WID, WID), WID)
        return r_buf.at[:, pl.ds(pl.multiple_of(xs * 16, 16), 16), cols]

    out_cp = []

    def rows(p, a):
        dx, dc = REL[a]
        xd, cd = lax.rem(x + dx, NX), lax.rem(c + dc, 2)
        base = pl.multiple_of((xd * 2 + cd) * (ROWS * 16), 32)
        got = dot(w_buf[pl.ds(base, ROWS * 16), :], x_buf[p])
        o_buf[p, a] = got.astype(BF).reshape(ROWS, 16, WID)
        if a < 7:
            cp = send(o_buf.at[p, a], place(p, x, c), x_s.at[p, a], x_r.at[p, a], at(dx=dx, dc=dc))
            pending.append(cp)
        else:
            cp = pltpu.make_async_copy(o_buf.at[p, a], place(p, x, c), loc.at[7 + p])
            out_cp.append(cp)
        cp.start()

    for p in range(1, PAIRS):
        rows(p - 1, 0)
        forward(p, 0, 2)
        rows(p - 1, 1)
        forward(p, 1, 2)
        rows(p - 1, 2)
        forward(p, 0, 3)
        rows(p - 1, 3)
        forward(p, 1, 3)
        if p + 1 < PAIRS:
            first(p + 1)
        rows(p - 1, 4)
        forward(p, 0, 4)
        rows(p - 1, 5)
        forward(p, 1, 4)
        rows(p - 1, 6)
        rows(p - 1, 7)
        finish(p)
    for a in range(8):
        rows(PAIRS - 1, a)

    own_li.wait()
    for cp in li_cp:
        cp.wait_recv()
    eye = (iota((TOK, TOK), 0) == iota((TOK, TOK), 1)).astype(BF)
    for g in range(8):
        lit[:, g * TOK : (g + 1) * TOK] = dot(lib[g], eye, ((0,), (0,))).astype(BF)

    load_e.wait()
    store_cp = []
    for p in range(PAIRS):
        for a in range(7):
            dx, dc = REL[a]
            xs, cs = lax.rem(x + NX - dx, NX), lax.rem(c + dc, 2)
            send(
                o_buf.at[p, a], place(p, xs, cs), x_s.at[p, a], x_r.at[p, a], at(dx=dx, dc=dc)
            ).wait_recv()
        out_cp[p].wait()
        for h in range(2):
            cols = pl.ds(h * 1024 + p * WID, WID)
            cp = pltpu.make_async_copy(r_buf.at[:, :, cols], grows.at[:, :, cols], loc.at[11 + 2 * p + h])
            cp.start()
            store_cp.append(cp)

        def score(r, carry, p=p):
            tot = jnp.zeros((64, 128), F32)
            for h in range(2):
                for t in range(WID // 128):
                    col = h * 1024 + p * WID + t * 128
                    a = r_buf[r, :, col : col + 128].astype(F32)
                    b = e_buf[r, :, col : col + 128].astype(F32)
                    tot = tot + a * b
            acc[r] = tot if p == 0 else acc[r] + tot
            return carry

        lax.fori_loop(0, ROWS, score, 0)

    total = jnp.zeros((64, 128), F32)
    for r in range(ROWS):
        total = jnp.where(iota((64, 128), 1) == r, jnp.sum(acc[r], axis=1, keepdims=True), total)
    s_out[...] = total.reshape(64, 1, 128)

    def sc(i):
        to = lax.rem(idx + i, 64)
        return send(s_out.at[to], t_in.at[idx], sc_s.at[i], sc_r.at[i], (y, to))

    def sc_start(i, carry):
        sc(i).start()
        return carry

    def sc_wait(i, carry):
        fr = lax.rem(idx + 64 - i, 64)
        send(s_out.at[fr], t_in.at[fr], sc_s.at[i], sc_r.at[i], (y, fr)).wait_recv()
        return carry

    lax.fori_loop(1, 64, sc_start, 0)
    t_in[pl.ds(idx, 1)] = s_out[pl.ds(idx, 1)]
    lax.fori_loop(1, 64, sc_wait, 0)

    back = t_in[...].reshape(64, 128)
    scaled = []
    for l in range(2):
        sl = own_slot[l * 64 : (l + 1) * 64, :]
        v = jnp.zeros((64, TOK), F32)
        for s in range(CAP):
            v = jnp.where(sl == float(s), back[:, l * CAP + s : l * CAP + s + 1], v)
        scaled.append(v)
    scaled = jnp.concatenate(scaled, axis=0)
    logits = scaled - own_gate[...] * jnp.sum(scaled, axis=0, keepdims=True)
    order = (2 * lax.rem(lane_row, 64) + lane_row // 64 == iota((TOK, TOK), 1)).astype(BF)
    glt[...] = dot(logits.astype(BF), order, ((0,), (0,))).astype(BF)

    gl_cp = []
    for i, (dy, dc) in enumerate(yc):
        cp = send(glt, glb.at[2 * y + c], gl_s.at[i], gl_r.at[i], at(dy=dy, dc=dc))
        cp.start()
        gl_cp.append(cp)
    glb[pl.ds(2 * y + c, 1)] = glt[...].reshape(1, TOK, EXP)
    gin[...] = dot(glt[...], rw[...], ((1,), (1,))).astype(BF)
    for cp in gl_cp:
        cp.wait_recv()
    part[...] = dot(lit[...], glb[...].reshape(8 * TOK, EXP))

    chip = x * NZ + z

    def chip_at(i):
        q = lax.rem(chip + i, 32)
        return q, (y, q * 2 + c)

    def rs_start(i, carry):
        q, to = chip_at(i)
        send(
            part.at[pl.ds(pl.multiple_of(q * 8, 8), 8)], rb.at[chip], rs_s.at[i], rs_r.at[i], to
        ).start()
        return carry

    def rs_wait(i, carry):
        q, to = chip_at(32 - i)
        send(
            part.at[pl.ds(pl.multiple_of(q * 8, 8), 8)], rb.at[q], rs_s.at[i], rs_r.at[i], to
        ).wait_recv()
        return carry

    lax.fori_loop(1, 32, rs_start, 0)
    rb[pl.ds(chip, 1)] = part[pl.ds(pl.multiple_of(chip * 8, 8), 8), :].reshape(1, 8, EXP)
    lax.fori_loop(1, 32, rs_wait, 0)
    fin[...] = jnp.sum(rb[...], axis=0)

    def a1_start(i, carry):
        q, to = chip_at(i)
        send(fin, ag.at[chip], a1_s.at[i], a1_r.at[i], to).start()
        return carry

    def a1_wait(i, carry):
        q, to = chip_at(32 - i)
        send(fin, ag.at[q], a1_s.at[i], a1_r.at[i], to).wait_recv()
        return carry

    lax.fori_loop(1, 32, a1_start, 0)
    ag[pl.ds(chip, 1)] = fin[...].reshape(1, 8, EXP)
    lax.fori_loop(1, 32, a1_wait, 0)
    half[...] = ag[...].reshape(256, EXP).astype(BF)

    a2_cp = []
    for i in range(1, NY):
        cp = send(half, agb.at[2 * y + c], a2_s.at[i], a2_r.at[i], at(dy=i))
        cp.start()
        a2_cp.append(cp)
    a3_cp = []

    def swap_part(i, g, src):
        cp = send(src, agb.at[g], a3_s.at[i], a3_r.at[i], at(dc=1))
        cp.start()
        a3_cp.append(cp)

    swap_part(0, 2 * y + c, half)
    agb[pl.ds(2 * y + c, 1)] = half[...].reshape(1, 256, EXP)
    for i in range(1, NY):
        ys = lax.rem(y + NY - i, NY)
        send(half, agb.at[2 * ys + c], a2_s.at[i], a2_r.at[i], at(dy=i)).wait_recv()
        swap_part(i, 2 * ys + c, agb.at[2 * ys + c])
    for i in range(NY):
        ys = lax.rem(y + NY - i, NY)
        g = 2 * ys + 1 - c
        send(half, agb.at[g], a3_s.at[i], a3_r.at[i], at(dc=1)).wait_recv()
    grout[...] = agb[...].reshape(D, EXP).astype(F32)

    for cp in swap + meta_cp + pending + li_cp + gl_cp + a2_cp + a3_cp:
        cp.wait_send()

    def sc_left(i, carry):
        sc(i).wait_send()
        return carry

    def rs_left(i, carry):
        q, to = chip_at(i)
        send(
            part.at[pl.ds(pl.multiple_of(q * 8, 8), 8)], rb.at[chip], rs_s.at[i], rs_r.at[i], to
        ).wait_send()
        send(fin, ag.at[chip], a1_s.at[i], a1_r.at[i], to).wait_send()
        return carry

    lax.fori_loop(1, 64, sc_left, 0)
    lax.fori_loop(1, 32, rs_left, 0)
    for cp in store_cp:
        cp.wait()


def body(grad_out, layer_input, router_weight, gate_probs, expert_ids, expert_out):
    meta = jnp.concatenate([expert_ids.T.astype(F32), gate_probs.T], axis=0)
    eo = expert_out[0].transpose(0, 2, 1, 3).reshape(ROWS, 64, D)
    vm, sem = pltpu.VMEM, pltpu.SemaphoreType.DMA
    hbm = pl.BlockSpec(memory_space=pl.ANY)
    vmem = pl.BlockSpec(memory_space=pltpu.VMEM)
    grows, gin, grout = pl.pallas_call(
        kernel,
        out_shape=(
            jax.ShapeDtypeStruct((ROWS, 64, D), BF),
            jax.ShapeDtypeStruct((TOK, D), BF),
            jax.ShapeDtypeStruct((D, EXP), F32),
        ),
        in_specs=[vmem, vmem, vmem, vmem, hbm],
        out_specs=(hbm, vmem, vmem),
        scratch_shapes=[
            vm((PAIRS, 16 * TOK, WID), BF),
            vm((PAIRS, 8, ROWS, 16, WID), BF),
            vm((8 * ROWS * 16, 16 * TOK), BF),
            vm((ROWS, 64, D), BF),
            vm((ROWS, 64, D), BF),
            vm((256, TOK), F32),
            vm((256, TOK), F32),
            vm((256, TOK), F32),
            vm((256, TOK), F32),
            vm((16, 16 * TOK), BF),
            vm((EXP, TOK), F32),
            vm((EXP, TOK), F32),
            vm((ROWS, 64, 128), F32),
            vm((64, 1, 128), F32),
            vm((64, 1, 128), F32),
            vm((8, TOK, WID), BF),
            vm((WID, 8 * TOK), BF),
            vm((TOK, EXP), BF),
            vm((8, TOK, EXP), BF),
            vm((WID, EXP), F32),
            vm((32, 8, EXP), F32),
            vm((8, EXP), F32),
            vm((32, 8, EXP), F32),
            vm((256, EXP), BF),
            vm((8, 256, EXP), BF),
            sem((19,)),
            sem((PAIRS,)), sem((PAIRS,)),
            sem((PAIRS, SUBS, 2, 4)), sem((PAIRS, SUBS, 2, 4)),
            sem((15,)), sem((15,)),
            sem((7,)), sem((7,)),
            sem((PAIRS, 7)), sem((PAIRS, 7)),
            sem((64,)), sem((64,)),
            sem((7,)), sem((7,)),
            sem((32,)), sem((32,)),
            sem((32,)), sem((32,)),
            sem((NY,)), sem((NY,)),
            sem((NY,)), sem((NY,)),
        ],
        compiler_params=pltpu.CompilerParams(
            collective_id=0, has_side_effects=True, vmem_limit_bytes=52 * 2**20
        ),
    )(grad_out, layer_input, router_weight, meta, eo)
    grows = grows.reshape(2, CAP, 64, D).transpose(0, 2, 1, 3)
    return grows[None], gin, grout


def solution(mesh):
    return jax.shard_map(
        body,
        mesh=mesh,
        in_specs=(
            P(("dp", "expert"), None),
            P(("dp", "expert"), None),
            P(),
            P(("dp", "expert"), None),
            P(("dp", "expert"), None),
            P("dp", "expert", None, None, None),
        ),
        out_specs=(P("dp", "expert", None, None, None), P(("dp", "expert"), None), P()),
        check_vma=False,
    )
```

time: 462 us -> 135 us (0.29)
  waiting for transfers between devices: 344 us -> 0 us
  Pallas kernels: 0 us -> 124 us
  local copies, waits for them, and re-layouts: 46.3 us -> 9.18 us
  starting transfers between devices: 29.9 us -> 0 us
  other arithmetic: 24.4 us -> 1.38 us
  between operations: 14.2 us -> 0.65 us
    psum x1 -> x0, waiting for transfers between devices: 233 us -> none  [body(): grad_router = lax.psum(weight_part, ('dp', 'expert'))]
    pallas_call x0 -> x1, Pallas kernels: none -> 124 us  [body(): pl.pallas_call(kernel, out_shape=(jax.ShapeDtypeStruct((ROWS, 64, D), BF)...]
    all_to_all x3 -> x0, waiting for transfers between devices: 111 us -> none  [the longest x1 102 us: body(): lax.all_to_all(send_rows, 'expert', split_axis=1, concat_axis=1, tiled=True)]
    all_to_all x3 -> x0, starting transfers between devices: 29.6 us -> none  [the longest x1 13.5 us: body(): lax.all_to_all(send_rows, 'expert', split_axis=1, concat_axis=1, tiled=True)]
    unnamed x23 -> x9, local copies, waits for them, and re-layouts: 24.4 us -> 9.18 us
    gather x2 -> x0, local copies, waits for them, and re-layouts: 9.85 us -> none  [body(): grad_gate = returned[which, owner, slot]]
    scatter x1 -> x0, local copies, waits for them, and re-layouts: 9.36 us -> none  [body(): jnp.zeros((local, devices, slots, width), jnp.bfloat16)]
    broadcast_in_dim x2 -> x0, other arithmetic: 8.94 us -> none  [the longest x1 8.24 us: body(): return (grad_y[None], grad_input, grad_router)]
  transfers between devices with their start and end apart: 4 -> 0, of which waited for: 3 -> 0; matrix products, arithmetic and copies ran while one was open for 8% -> 0% of each run, Pallas kernels for 0% -> 0%
where the time goes in v1:
time: 135 us
  Pallas kernels  124 us (92%)
  local copies, waits for them, and re-layouts  9.18 us (7%)
  other arithmetic  1.38 us (1%)
    pallas_call x1, Pallas kernels, body(): pl.pallas_call(kernel, out_shape=(jax.ShapeDtypeStruct((ROWS, 64, D), BF)...  124 us
    unnamed x9, local copies, waits for them, and re-layouts  9.18 us

profile of v1, /device:TPU:1, one launch (start us, length us, event | category | flops | bytes accessed | tf_op | source)
XLA Modules:
  0.0 135.0 jit_solution(16167279148287785398)
XLA Ops:
  0.6 0.7 convert_bitcast_fusion
  1.3 0.7 pad_maximum_fusion.meta
  2.0 0.0 copy-start
  2.0 1.0 copy-done
  3.1 0.0 copy-start.1
  3.1 1.0 copy-done.1
  4.1 123.8 %shard_map.85 = (bf16[18,64,2048]{2,1,0:T(8,128)(2,1)}, bf16[128,2048]{1,0:T(8,128)(2,1)S(1)}, f32[2048,128]{1,0:T(8,128)}) custom-call(bf16[128,2048]{1,0:T(8,128)(2,1)S(1)} %copy-done, bf16[128,2048]{1,0:T(8,128)(2,1)S(1)} %copy-done.1, bf16[2048,128]{1,0:T(8,128)(2,1)} %rw.1, f32[16,128]{1,0:T(8,128)S(1)} %pad_maximum_fusion.meta, ...), custom_call_target="tpu_custom_call" | custom-call | tf_op jit(solution)/shard_map/pallas_call | solution.py:420
  127.9 0.0 copy-start.2
  127.9 5.3 %copy.12 = bf16[1,2,64,9,2048]{4,2,3,1,0:T(8,128)(2,1)} copy(bf16[1,2,64,9,2048]{4,2,3,1,0:T(8,128)(2,1)} %bitcast.14) | data formatting | bytes 9437184
  133.3 0.8 copy.13
  134.1 0.0 copy-done.2
  134.1 1.0 copy.14
Async XLA Ops:
  2.0 1.0 copy-start
  3.1 1.0 copy-start.1
  127.9 6.1 %copy-start.2 = (f32[2048,128]{1,0:T(8,128)S(1)}, f32[2048,128]{1,0:T(8,128)}, u32[]{:S(2)}) copy-start(f32[2048,128]{1,0:T(8,128)} %get-tuple-element.14) | copy-start | bytes 3145732

commit v2 on v1

v2 whole, which is shorter than its diff:
```python
import jax
import jax.numpy as jnp
from jax import lax
from jax.experimental import pallas as pl
from jax.experimental.pallas import tpu as pltpu
from jax.sharding import PartitionSpec as P

MESH = pl.DeviceIdType.MESH
BF, F32 = jnp.bfloat16, jnp.float32
NX, NZ, NY = 4, 8, 4
D, TOK, TOP, EXP, CAP = 2048, 128, 8, 128, 9
ROWS = 2 * CAP
UNITS, UW, WID = 8, 128, 256
HOPS = ((4, 3), (3, 4))
STEP, HOP = 5.8, 3.3
REL = ((2, 0), (2, 1), (1, 0), (3, 0), (1, 1), (3, 1), (0, 1), (0, 0))


def iota(shape, axis):
    return lax.broadcasted_iota(jnp.int32, shape, axis)


def dot(a, b, dims=((1,), (0,))):
    return lax.dot_general(a, b, (dims, ((), ())), preferred_element_type=F32)


def earlier():
    return (iota((TOK, TOK), 0) < iota((TOK, TOK), 1)).astype(BF)


def kernel(
    go, li, rw_in, ids_in, gates_in, eo, grows, gin_out, agb_out,
    x_buf, f_buf, o_buf, w_buf, r_buf, gin, agb, e_buf, rw, ids_own, gates_own, meta, mb, slots, gates, m_buf,
    own_slot, own_gate, acc, s_out, t_in, lib, lit, glt, glb, part, rb, fin, ag, half,
    loc, xch_s, xch_r, ring_s, ring_r, meta_s, meta_r, li_s, li_r, x_s, x_r,
    sc_s, sc_r, gl_s, gl_r, rs_s, rs_r, a1_s, a1_r, a2_s, a2_r, a3_s, a3_r,
):
    y = lax.axis_index("dp")
    idx = lax.axis_index("expert")
    x, z, c = idx // 16, (idx // 2) % NZ, idx % 2

    def at(dx=0, dy=0, dz=0, dc=0):
        xx, zz, cc = lax.rem(x + dx, NX), lax.rem(z + dz, NZ), lax.rem(c + dc, 2)
        return (lax.rem(y + dy, NY), xx * 16 + zz * 2 + cc)

    def bulk(ref, n, s):
        pltpu.make_async_copy(ref.at[pl.ds(0, n)], ref.at[pl.ds(0, n)], s).wait()

    def send(src, dst, ss, rs, to):
        return pltpu.make_async_remote_copy(
            src_ref=src, dst_ref=dst, send_sem=ss, recv_sem=rs, device_id=to, device_id_type=MESH
        )

    load_ids = pltpu.make_async_copy(ids_in, ids_own, loc.at[6])
    load_ids.start()
    load_gates = pltpu.make_async_copy(gates_in, gates_own, loc.at[11])
    load_gates.start()
    load_e = pltpu.make_async_copy(eo, e_buf, loc.at[0])
    load_e.start()
    own_half = []
    for u in range(UNITS):
        cols = pl.ds(pl.multiple_of(c * 1024 + u * UW, UW), UW)
        cp = pltpu.make_async_copy(go.at[:, cols], x_buf.at[u, 2 * z + c], loc.at[13 + u])
        cp.start()
        own_half.append(cp)
    own_li = pltpu.make_async_copy(
        li.at[:, pl.ds(pl.multiple_of((2 * y + c) * WID, WID), WID)], lib.at[2 * y + c], loc.at[5]
    )
    own_li.start()
    load_rw = pltpu.make_async_copy(rw_in, rw, loc.at[12])
    load_rw.start()

    barrier = pltpu.get_barrier_semaphore()
    zc = [(dz, dc) for dz in range(NZ) for dc in range(2) if dz or dc]
    yc = [(dy, dc) for dy in range(NY) for dc in range(2) if dy or dc]
    greet = [dict(dz=a, dc=b) for a, b in zc]
    greet += [dict(dx=a, dc=b) for a, b in REL if a]
    greet += [dict(dy=a, dc=b) for a, b in yc if a]
    for g in greet:
        pl.semaphore_signal(barrier, inc=1, device_id=at(**g), device_id_type=MESH)
    load_ids.wait()
    load_gates.wait()
    meta[0:TOP, :] = ids_own[...].astype(F32).astype(BF)
    meta[TOP:, :] = gates_own[...].astype(BF)
    mb[pl.ds(2 * z + c, 1)] = meta[...].reshape(1, 2 * TOP, TOK)
    pl.semaphore_wait(barrier, len(greet))

    pending = []

    swap = []
    for u in range(UNITS):
        cols = pl.ds(pl.multiple_of((1 - c) * 1024 + u * UW, UW), UW)
        swap.append(
            send(go.at[:, cols], x_buf.at[u, 2 * z + c], xch_s.at[u], xch_r.at[u], at(dc=1))
        )
    swap[0].start()
    swap[1].start()

    def came(d, h):
        return lax.rem(z + (NZ - h if d == 0 else h), NZ)

    def ring(u, d, h):
        blk = x_buf.at[u, pl.ds(2 * came(d, h - 1), 2)]
        return send(
            blk, blk, ring_s.at[u, d, h - 1], ring_r.at[u, d, h - 1],
            at(dz=1 if d == 0 else NZ - 1),
        )

    def landed(u, d, h):
        blk = x_buf.at[u, pl.ds(2 * came(d, h), 2)]
        send(
            blk, blk, ring_s.at[u, d, h - 1], ring_r.at[u, d, h - 1],
            at(dz=1 if d == 0 else NZ - 1),
        ).wait_recv()

    def hop(u, h):
        if h == 0:
            own_half[u].wait()
            swap[u].wait_recv()
        for d in range(2):
            if 0 < h <= HOPS[u % 2][d]:
                landed(u, d, h)
            if h < HOPS[u % 2][d]:
                cp = ring(u, d, h + 1)
                cp.start()
                pending.append(cp)

    steps = sorted((u * STEP + h * HOP, u, h) for u in range(UNITS) for h in range(5))
    steps = [(u, h) for _, u, h in steps]
    hop(*steps[0])

    meta_cp = []
    for i, (dz, dc) in enumerate(zc):
        cp = send(meta, mb.at[2 * z + c], meta_s.at[i], meta_r.at[i], at(dz=dz, dc=dc))
        cp.start()
        meta_cp.append(cp)
    for u in range(2, UNITS):
        swap[u].start()

    lane_row = iota((TOK, TOK), 0)
    expert = 2 * lax.rem(lane_row, 64) + lane_row // 64
    named = jnp.zeros((EXP, TOK), F32)
    gate = jnp.zeros((EXP, TOK), F32)
    for k in range(TOP):
        hit = ids_own[k : k + 1, :] == expert
        named = jnp.where(hit, 1.0, named)
        gate = jnp.where(hit, gates_own[k : k + 1, :], gate)
    before = dot(named.astype(BF), earlier())
    own_slot[...] = jnp.where(named > 0, before, 99.0)
    own_gate[...] = gate

    li_cp = []
    for i, (dy, dc) in enumerate(yc):
        g = 2 * lax.rem(y + dy, NY) + lax.rem(c + dc, 2)
        cp = send(
            li.at[:, pl.ds(pl.multiple_of(g * WID, WID), WID)], lib.at[2 * y + c],
            li_s.at[i], li_r.at[i], at(dy=dy, dc=dc),
        )
        li_cp.append(cp)

    def tables():
        for cp in meta_cp:
            cp.wait_recv()
        row = iota((16, TOK), 0)
        here = (row // 4) * 32 + z * 4 + lax.rem(row, 4)
        for j in range(16):
            ids = mb[j, 0:TOP, :].astype(F32).astype(jnp.int32)
            gts = mb[j, TOP:, :].astype(F32)
            nm = jnp.zeros((16, TOK), F32)
            gt = jnp.zeros((16, TOK), F32)
            for k in range(TOP):
                hit = ids[k : k + 1, :] == here
                nm = jnp.where(hit, 1.0, nm)
                gt = jnp.where(hit, gts[k : k + 1, :], gt)
            m_buf[j * 16 : (j + 1) * 16, :] = nm
            gates[j * 16 : (j + 1) * 16, :] = gt
        bef = dot(m_buf[...].astype(BF), earlier())
        slots[...] = jnp.where(m_buf[...] > 0, bef, 99.0)

        def one(j, carry):
            base = pl.multiple_of(j * 16, 16)
            sl = slots[pl.ds(base, 16), :]
            gt = gates[pl.ds(base, 16), :]
            for s in range(CAP):
                w_buf[j, s * 16 : (s + 1) * 16, :] = jnp.where(sl == float(s), gt, 0.0).astype(BF)
            return carry

        lax.fori_loop(0, 16, one, 0)

    def block(u, zb):
        for i in range(2):
            j = 2 * zb + i
            got = dot(w_buf[j], x_buf[u, j])
            for s in range(CAP):
                f_buf[u % 4, pl.ds(s * 16 + j, 16, stride=CAP * 16), :] = got[s * 16 : (s + 1) * 16, :]

    def place(u, xs, cs):
        cols = pl.ds(pl.multiple_of(cs * 1024 + u * UW, UW), UW)
        return r_buf.at[:, pl.ds(pl.multiple_of(xs * 16, 16), 16), cols]

    out_cp = []

    def rows(u, a):
        dx, dc = REL[a]
        xd, cd = lax.rem(x + dx, NX), lax.rem(c + dc, 2)
        base = pl.multiple_of((xd * 2 + cd) * (ROWS * 16), 32)
        o_buf[u, a] = f_buf[u % 4, pl.ds(base, ROWS * 16), :].astype(BF).reshape(ROWS, 16, UW)
        if a < 7:
            cp = send(o_buf.at[u, a], place(u, x, c), x_s.at[u, a], x_r.at[u, a], at(dx=dx, dc=dc))
            pending.append(cp)
        else:
            cp = pltpu.make_async_copy(o_buf.at[u, a], place(u, x, c), loc.at[21 + u])
            out_cp.append(cp)
        cp.start()

    def work(u, h):
        if h == 0:
            block(u, z)
        for d in range(2):
            if 0 < h <= HOPS[u % 2][d]:
                block(u, came(d, h))
        if h == 4:
            for a in range(8):
                rows(u, a)

    late = [steps[0]]
    for n, (u, h) in enumerate(steps[1:]):
        hop(u, h)
        late.append((u, h))
        if n == 2:
            for cp in li_cp:
                cp.start()
            tables()
        if n >= 2:
            for q in late:
                work(*q)
            late = []

    own_li.wait()
    for cp in li_cp:
        cp.wait_recv()
    eye = (iota((TOK, TOK), 0) == iota((TOK, TOK), 1)).astype(BF)
    for g in range(8):
        lit[:, g * TOK : (g + 1) * TOK] = dot(lib[g], eye, ((0,), (0,))).astype(BF)

    load_e.wait()
    store_cp = []
    for u in range(UNITS):
        for a in range(7):
            dx, dc = REL[a]
            xs, cs = lax.rem(x + NX - dx, NX), lax.rem(c + dc, 2)
            send(
                o_buf.at[u, a], place(u, xs, cs), x_s.at[u, a], x_r.at[u, a], at(dx=dx, dc=dc)
            ).wait_recv()
        out_cp[u].wait()
        for h in range(2):
            cols = pl.ds(h * 1024 + u * UW, UW)
            cp = pltpu.make_async_copy(r_buf.at[:, :, cols], grows.at[:, :, cols], loc.at[29 + 2 * u + h])
            cp.start()
            store_cp.append(cp)

        def score(r, carry, u=u):
            tot = jnp.zeros((64, 128), F32)
            for h in range(2):
                col = h * 1024 + u * UW
                a = r_buf[r, :, col : col + 128].astype(F32)
                b = e_buf[r, :, col : col + 128].astype(F32)
                tot = tot + a * b
            acc[r] = tot if u == 0 else acc[r] + tot
            return carry

        lax.fori_loop(0, ROWS, score, 0)

    total = jnp.zeros((64, 128), F32)
    for r in range(ROWS):
        total = jnp.where(iota((64, 128), 1) == r, jnp.sum(acc[r], axis=1, keepdims=True), total)
    s_out[...] = total.reshape(64, 1, 128)

    def sc(i):
        to = lax.rem(idx + i, 64)
        return send(s_out.at[to], t_in.at[idx], sc_s, sc_r, (y, to))

    def sc_start(i, carry):
        sc(i).start()
        return carry

    lax.fori_loop(1, 64, sc_start, 0)
    t_in[pl.ds(idx, 1)] = s_out[pl.ds(idx, 1)]
    for cp in swap + meta_cp + pending + li_cp:
        cp.wait_send()
    bulk(t_in, 63, sc_r)

    back = t_in[...].reshape(64, 128)
    scaled = []
    for l in range(2):
        sl = own_slot[l * 64 : (l + 1) * 64, :]
        v = jnp.zeros((64, TOK), F32)
        for s in range(CAP):
            v = jnp.where(sl == float(s), back[:, l * CAP + s : l * CAP + s + 1], v)
        scaled.append(v)
    scaled = jnp.concatenate(scaled, axis=0)
    logits = scaled - own_gate[...] * jnp.sum(scaled, axis=0, keepdims=True)
    order = (2 * lax.rem(lane_row, 64) + lane_row // 64 == iota((TOK, TOK), 1)).astype(BF)
    glt[...] = dot(logits.astype(BF), order, ((0,), (0,))).astype(BF)

    gl_cp = []
    for i, (dy, dc) in enumerate(yc):
        cp = send(glt, glb.at[2 * y + c], gl_s.at[i], gl_r.at[i], at(dy=dy, dc=dc))
        cp.start()
        gl_cp.append(cp)
    glb[pl.ds(2 * y + c, 1)] = glt[...].reshape(1, TOK, EXP)
    load_rw.wait()
    gin[...] = dot(glt[...], rw[...], ((1,), (1,))).astype(BF)
    cp = pltpu.make_async_copy(gin, gin_out, loc.at[1])
    cp.start()
    store_cp.append(cp)
    for cp in gl_cp:
        cp.wait_recv()
    part[...] = dot(lit[...], glb[...].reshape(8 * TOK, EXP))

    chip = x * NZ + z

    def chip_at(i):
        q = lax.rem(chip + i, 32)
        return q, (y, q * 2 + c)

    def rs_start(i, carry):
        q, to = chip_at(i)
        send(
            part.at[pl.ds(pl.multiple_of(q * 8, 8), 8)], rb.at[chip], rs_s, rs_r, to
        ).start()
        return carry

    lax.fori_loop(1, 32, rs_start, 0)
    rb[pl.ds(chip, 1)] = part[pl.ds(pl.multiple_of(chip * 8, 8), 8), :].reshape(1, 8, EXP)
    bulk(s_out, 63, sc_s)
    for cp in gl_cp:
        cp.wait_send()
    bulk(rb, 31, rs_r)
    fin[...] = jnp.sum(rb[...], axis=0)

    def a1_start(i, carry):
        q, to = chip_at(i)
        send(fin, ag.at[chip], a1_s, a1_r, to).start()
        return carry

    lax.fori_loop(1, 32, a1_start, 0)
    ag[pl.ds(chip, 1)] = fin[...].reshape(1, 8, EXP)
    bulk(rb, 31, rs_s)
    bulk(ag, 31, a1_r)
    half[...] = ag[...].reshape(256, EXP).astype(BF)

    a2_cp = []
    for i in range(1, NY):
        cp = send(half, agb.at[2 * y + c], a2_s.at[i], a2_r.at[i], at(dy=i))
        cp.start()
        a2_cp.append(cp)
    a3_cp = []

    def swap_part(i, g, src):
        cp = send(src, agb.at[g], a3_s.at[i], a3_r.at[i], at(dc=1))
        cp.start()
        a3_cp.append(cp)

    swap_part(0, 2 * y + c, half)
    agb[pl.ds(2 * y + c, 1)] = half[...].reshape(1, 256, EXP)
    bulk(ag, 31, a1_s)
    for cp in store_cp:
        cp.wait()
    for i in range(1, NY):
        ys = lax.rem(y + NY - i, NY)
        send(half, agb.at[2 * ys + c], a2_s.at[i], a2_r.at[i], at(dy=i)).wait_recv()
        swap_part(i, 2 * ys + c, agb.at[2 * ys + c])
    for i in range(NY):
        ys = lax.rem(y + NY - i, NY)
        g = 2 * ys + 1 - c
        send(half, agb.at[g], a3_s.at[i], a3_r.at[i], at(dc=1)).wait_recv()

    store = pltpu.make_async_copy(agb, agb_out, loc.at[0])
    store.start()
    for cp in a2_cp + a3_cp:
        cp.wait_send()
    store.wait()


def writer(rows_in, gin_in, agb_in, grows, gin_out, grout, rows, gin, parts, wide, loc, sto):
    pieces = [(rows_in.at[pl.ds(3 * i, 3)], rows.at[pl.ds(3 * i, 3)], grows.at[pl.ds(3 * i, 3)]) for i in range(6)]
    pieces.append((gin_in, gin, gin_out))
    load = pltpu.make_async_copy(agb_in, parts, loc.at[7])
    load.start()
    loads = [pltpu.make_async_copy(a, b, loc.at[i]) for i, (a, b, _) in enumerate(pieces)]
    stores = [pltpu.make_async_copy(b, c, sto.at[i]) for i, (_, b, c) in enumerate(pieces)]
    for cp in loads:
        cp.start()
    load.wait()
    wide[...] = parts[...].reshape(D, EXP).astype(F32)
    stores.append(pltpu.make_async_copy(wide, grout, sto.at[7]))
    stores[7].start()
    for i in range(7):
        loads[i].wait()
        stores[i].start()
    for cp in stores:
        cp.wait()


def body(grad_out, layer_input, router_weight, gate_probs, expert_ids, expert_out):
    eo = expert_out[0].transpose(0, 2, 1, 3).reshape(ROWS, 64, D)
    vm, sem = pltpu.VMEM, pltpu.SemaphoreType.DMA
    hbm = pl.BlockSpec(memory_space=pltpu.HBM)
    results = pl.pallas_call(
        kernel,
        out_shape=(
            jax.ShapeDtypeStruct((ROWS, 64, D), BF),
            jax.ShapeDtypeStruct((TOK, D), BF),
            jax.ShapeDtypeStruct((8, 256, EXP), BF),
        ),
        in_specs=[hbm] * 6,
        out_specs=(hbm, hbm, hbm),
        scratch_shapes=[
            vm((UNITS, 16, TOK, UW), BF),
            vm((4, 8 * ROWS * 16, UW), F32),
            vm((UNITS, 8, ROWS, 16, UW), BF),
            vm((16, CAP * 16, TOK), BF),
            vm((ROWS, 64, D), BF),
            vm((TOK, D), BF),
            vm((8, 256, EXP), BF),
            vm((ROWS, 64, D), BF),
            vm((D, EXP), BF),
            vm((TOP, TOK), jnp.int32),
            vm((TOP, TOK), F32),
            vm((2 * TOP, TOK), BF),
            vm((16, 2 * TOP, TOK), BF),
            vm((256, TOK), F32),
            vm((256, TOK), F32),
            vm((256, TOK), F32),
            vm((EXP, TOK), F32),
            vm((EXP, TOK), F32),
            vm((ROWS, 64, 128), F32),
            vm((64, 1, 128), F32),
            vm((64, 1, 128), F32),
            vm((8, TOK, WID), BF),
            vm((WID, 8 * TOK), BF),
            vm((TOK, EXP), BF),
            vm((8, TOK, EXP), BF),
            vm((WID, EXP), F32),
            vm((32, 8, EXP), F32),
            vm((8, EXP), F32),
            vm((32, 8, EXP), F32),
            vm((256, EXP), BF),
            sem((45,)),
            sem((UNITS,)), sem((UNITS,)),
            sem((UNITS, 2, 4)), sem((UNITS, 2, 4)),
            sem((15,)), sem((15,)),
            sem((7,)), sem((7,)),
            sem((UNITS, 7)), sem((UNITS, 7)),
            sem, sem,
            sem((7,)), sem((7,)),
            sem, sem,
            sem, sem,
            sem((NY,)), sem((NY,)),
            sem((NY,)), sem((NY,)),
        ],
        compiler_params=pltpu.CompilerParams(
            collective_id=0, has_side_effects=True, vmem_limit_bytes=57 * 2**20
        ),
    )(grad_out, layer_input, router_weight, expert_ids.T, gate_probs.T, eo)
    grows, gin, grout = pl.pallas_call(
        writer,
        out_shape=(
            jax.ShapeDtypeStruct((ROWS, 64, D), BF),
            jax.ShapeDtypeStruct((TOK, D), BF),
            jax.ShapeDtypeStruct((D, EXP), F32),
        ),
        in_specs=[hbm] * 3,
        out_specs=(hbm, hbm, hbm),
        scratch_shapes=[
            vm((ROWS, 64, D), BF), vm((TOK, D), BF), vm((8, 256, EXP), BF), vm((D, EXP), F32),
            sem((8,)), sem((8,)),
        ],
        compiler_params=pltpu.CompilerParams(vmem_limit_bytes=57 * 2**20),
    )(*results)
    grows = grows.reshape(2, CAP, 64, D).transpose(0, 2, 1, 3)
    return grows[None], gin, grout


def solution(mesh):
    return jax.shard_map(
        body,
        mesh=mesh,
        in_specs=(
            P(("dp", "expert"), None),
            P(("dp", "expert"), None),
            P(),
            P(("dp", "expert"), None),
            P(("dp", "expert"), None),
            P("dp", "expert", None, None, None),
        ),
        out_specs=(P("dp", "expert", None, None, None), P(("dp", "expert"), None), P()),
        check_vma=False,
    )
```

time: 135 us -> 120 us (0.89)
  local copies, waits for them, and re-layouts: 9.18 us -> 0 us
  Pallas kernels: 124 us -> 120 us
  other arithmetic: 1.38 us -> 0 us
    pallas_call x1, Pallas kernels: 124 us -> 115 us  [body(): pl.pallas_call(kernel, out_shape=(jax.ShapeDtypeStruct((ROWS, 64, D), BF)...]
    unnamed x9 -> x0, local copies, waits for them, and re-layouts: 9.18 us -> none
    pallas_call x0 -> x1, Pallas kernels: none -> 5.05 us  [body(): pl.pallas_call(writer, out_shape=(jax.ShapeDtypeStruct((ROWS, 64, D), BF)...]
where the time goes in v2:
time: 120 us
  Pallas kernels  120 us (100%)
    pallas_call x1, Pallas kernels, body(): pl.pallas_call(kernel, out_shape=(jax.ShapeDtypeStruct((ROWS, 64, D), BF)...  115 us
    pallas_call x1, Pallas kernels, body(): pl.pallas_call(writer, out_shape=(jax.ShapeDtypeStruct((ROWS, 64, D), BF)...  5.05 us

profile of v2, /device:TPU:1, one launch (start us, length us, event | category | flops | bytes accessed | tf_op | source)
XLA Modules:
  0.0 120.3 jit_solution(10815118637927239378)
XLA Ops:
  0.6 114.6 %shard_map.85 = (bf16[18,64,2048]{2,1,0:T(8,128)(2,1)}, bf16[128,2048]{1,0:T(8,128)(2,1)}, bf16[8,256,128]{2,1,0:T(8,128)(2,1)}) custom-call(bf16[128,2048]{1,0:T(8,128)(2,1)} %go.1, bf16[128,2048]{1,0:T(8,128)(2,1)} %li.1, bf16[2048,128]{1,0:T(8,128)(2,1)} %rw_in.1, s32[8,128]{1,0:T(8,128)} %bitcast.13, f32[8,128]{1,0:T(8,128)} %bitcast.14, ...), custom_call_target="tpu_custom_call" | custom-call | tf_op jit(solution)/shard_map/pallas_call | solution.py:410
  115.3 5.0 %shard_map.86 = (bf16[18,64,2048]{2,1,0:T(8,128)(2,1)}, bf16[128,2048]{1,0:T(8,128)(2,1)}, f32[2048,128]{1,0:T(8,128)}) custom-call(bf16[18,64,2048]{2,1,0:T(8,128)(2,1)} %get-tuple-element.9.rows_in, bf16[128,2048]{1,0:T(8,128)(2,1)} %get-tuple-element.10.gin_in, bf16[8,256,128]{2,1,0:T(8,128)(2,1)} %get-tuple-element.11.agb_in), custom_call_target="tpu_custom_call" | custom-call | tf_op jit(solution)/shard_map/pallas_call | solution.py:467

commit v3 on v2

--- a/solution.py
+++ b/solution.py
@@ -11,8 +11,12 @@
 D, TOK, TOP, EXP, CAP = 2048, 128, 8, 128, 9
 ROWS = 2 * CAP
 UNITS, UW, WID = 8, 128, 256
+RING = 7
 HOPS = ((4, 3), (3, 4))
-STEP, HOP = 5.8, 3.3
+STEP, HOP = 4.8, 3.3
+ORDER = (0, 1, 2, 3, 4, 5, 7, 6)
+ACROSS = tuple((dz, dc) for dz in (4, 3, 5, 2, 6, 1, 7) for dc in range(2)) + ((0, 1),)
+SPREAD = (0, 0, 0, 0, 0, 5, 10)
 REL = ((2, 0), (2, 1), (1, 0), (3, 0), (1, 1), (3, 1), (0, 1), (0, 0))
 
 
@@ -30,9 +34,9 @@
 
 def kernel(
     go, li, rw_in, ids_in, gates_in, eo, grows, gin_out, agb_out,
-    x_buf, f_buf, o_buf, w_buf, r_buf, gin, agb, e_buf, rw, ids_own, gates_own, meta, mb, slots, gates, m_buf,
+    x_buf, f_buf, o_buf, w_buf, r_buf, gin, agb, e_buf, rw, ids_own, gates_own, meta, mb, slots, gates, m_buf, mb2, g2_buf, w2_buf, f2_buf, o2_buf, h_in, turn, order,
     own_slot, own_gate, acc, s_out, t_in, lib, lit, glt, glb, part, rb, fin, ag, half,
-    loc, xch_s, xch_r, ring_s, ring_r, meta_s, meta_r, li_s, li_r, x_s, x_r,
+    loc, xch_s, xch_r, ring_s, ring_r, meta_s, meta_r, li_s, li_r, x_s, x_r, h_s, h_r, h2_s, h2_r, h3_s, h3_r,
     sc_s, sc_r, gl_s, gl_r, rs_s, rs_r, a1_s, a1_r, a2_s, a2_r, a3_s, a3_r,
 ):
     y = lax.axis_index("dp")
@@ -46,6 +50,9 @@
     def bulk(ref, n, s):
         pltpu.make_async_copy(ref.at[pl.ds(0, n)], ref.at[pl.ds(0, n)], s).wait()
 
+    def taken(ref, s):
+        pltpu.make_async_copy(ref, ref, s).wait()
+
     def send(src, dst, ss, rs, to):
         return pltpu.make_async_remote_copy(
             src_ref=src, dst_ref=dst, send_sem=ss, recv_sem=rs, device_id=to, device_id_type=MESH
@@ -53,21 +60,21 @@
 
     load_ids = pltpu.make_async_copy(ids_in, ids_own, loc.at[6])
     load_ids.start()
-    load_gates = pltpu.make_async_copy(gates_in, gates_own, loc.at[11])
+    load_gates = pltpu.make_async_copy(gates_in, gates_own, loc.at[2])
     load_gates.start()
     load_e = pltpu.make_async_copy(eo, e_buf, loc.at[0])
     load_e.start()
     own_half = []
     for u in range(UNITS):
         cols = pl.ds(pl.multiple_of(c * 1024 + u * UW, UW), UW)
-        cp = pltpu.make_async_copy(go.at[:, cols], x_buf.at[u, 2 * z + c], loc.at[13 + u])
+        cp = pltpu.make_async_copy(go.at[:, cols], x_buf.at[u, 2 * z + c], loc.at[7 + u])
         cp.start()
         own_half.append(cp)
     own_li = pltpu.make_async_copy(
         li.at[:, pl.ds(pl.multiple_of((2 * y + c) * WID, WID), WID)], lib.at[2 * y + c], loc.at[5]
     )
     own_li.start()
-    load_rw = pltpu.make_async_copy(rw_in, rw, loc.at[12])
+    load_rw = pltpu.make_async_copy(rw_in, rw, loc.at[3])
     load_rw.start()
 
     barrier = pltpu.get_barrier_semaphore()
@@ -85,15 +92,15 @@
     mb[pl.ds(2 * z + c, 1)] = meta[...].reshape(1, 2 * TOP, TOK)
     pl.semaphore_wait(barrier, len(greet))
 
-    pending = []
 
     swap = []
     for u in range(UNITS):
         cols = pl.ds(pl.multiple_of((1 - c) * 1024 + u * UW, UW), UW)
         swap.append(
-            send(go.at[:, cols], x_buf.at[u, 2 * z + c], xch_s.at[u], xch_r.at[u], at(dc=1))
+            send(go.at[:, cols], x_buf.at[u, 2 * z + c], xch_s, xch_r.at[u], at(dc=1))
         )
     swap[0].start()
+    swap[RING].start()
     swap[1].start()
 
     def came(d, h):
@@ -102,14 +109,14 @@
     def ring(u, d, h):
         blk = x_buf.at[u, pl.ds(2 * came(d, h - 1), 2)]
         return send(
-            blk, blk, ring_s.at[u, d, h - 1], ring_r.at[u, d, h - 1],
+            blk, blk, ring_s, ring_r.at[u, d, h - 1],
             at(dz=1 if d == 0 else NZ - 1),
         )
 
     def landed(u, d, h):
         blk = x_buf.at[u, pl.ds(2 * came(d, h), 2)]
         send(
-            blk, blk, ring_s.at[u, d, h - 1], ring_r.at[u, d, h - 1],
+            blk, blk, ring_s, ring_r.at[u, d, h - 1],
             at(dz=1 if d == 0 else NZ - 1),
         ).wait_recv()
 
@@ -123,19 +130,27 @@
             if h < HOPS[u % 2][d]:
                 cp = ring(u, d, h + 1)
                 cp.start()
-                pending.append(cp)
-
-    steps = sorted((u * STEP + h * HOP, u, h) for u in range(UNITS) for h in range(5))
+
+    steps = sorted((u * STEP + h * HOP, u, h) for u in range(RING) for h in range(5))
     steps = [(u, h) for _, u, h in steps]
     hop(*steps[0])
 
-    meta_cp = []
     for i, (dz, dc) in enumerate(zc):
-        cp = send(meta, mb.at[2 * z + c], meta_s.at[i], meta_r.at[i], at(dz=dz, dc=dc))
-        cp.start()
-        meta_cp.append(cp)
-    for u in range(2, UNITS):
+        cp = send(meta, mb.at[2 * z + c], meta_s, meta_r, at(dz=dz, dc=dc))
+        cp.start()
+    for u in range(2, RING):
         swap[u].start()
+
+    own_half[RING].wait()
+    swap[RING].wait_recv()
+    for i in range(1, NX):
+        cp = send(x_buf.at[RING, pl.ds(2 * z, 2)], g2_buf.at[pl.ds(2 * x, 2)], h_s, h_r, at(dx=i))
+        cp.start()
+    xc = [(dx, dc) for dx, dc in REL if dx]
+    for i, (dx, dc) in enumerate(xc):
+        cp = send(meta, mb2.at[2 * x + c], h2_s, h2_r, at(dx=dx, dc=dc))
+        cp.start()
+    g2_buf[pl.ds(2 * x, 2)] = x_buf[RING, pl.ds(2 * z, 2)]
 
     lane_row = iota((TOK, TOK), 0)
     expert = 2 * lax.rem(lane_row, 64) + lane_row // 64
@@ -154,13 +169,12 @@
         g = 2 * lax.rem(y + dy, NY) + lax.rem(c + dc, 2)
         cp = send(
             li.at[:, pl.ds(pl.multiple_of(g * WID, WID), WID)], lib.at[2 * y + c],
-            li_s.at[i], li_r.at[i], at(dy=dy, dc=dc),
+            li_s, li_r, at(dy=dy, dc=dc),
         )
         li_cp.append(cp)
 
     def tables():
-        for cp in meta_cp:
-            cp.wait_recv()
+        bulk(mb, 15, meta_r)
         row = iota((16, TOK), 0)
         here = (row // 4) * 32 + z * 4 + lax.rem(row, 4)
         for j in range(16):
@@ -206,12 +220,71 @@
         base = pl.multiple_of((xd * 2 + cd) * (ROWS * 16), 32)
         o_buf[u, a] = f_buf[u % 4, pl.ds(base, ROWS * 16), :].astype(BF).reshape(ROWS, 16, UW)
         if a < 7:
-            cp = send(o_buf.at[u, a], place(u, x, c), x_s.at[u, a], x_r.at[u, a], at(dx=dx, dc=dc))
-            pending.append(cp)
+            cp = send(o_buf.at[u, a], place(u, x, c), x_s, x_r.at[u], at(dx=dx, dc=dc))
         else:
-            cp = pltpu.make_async_copy(o_buf.at[u, a], place(u, x, c), loc.at[21 + u])
+            cp = pltpu.make_async_copy(o_buf.at[u, a], place(u, x, c), loc.at[15 + u])
             out_cp.append(cp)
         cp.start()
+
+    def across():
+        bulk(g2_buf, 6, h_r)
+        bulk(mb2, 6, h2_r)
+        mb2[pl.ds(2 * x, 2)] = mb[pl.ds(2 * z, 2)]
+        here = x * 32 + iota((32, TOK), 0)
+        for j in range(8):
+            ids = mb2[j, 0:TOP, :].astype(F32).astype(jnp.int32)
+            gts = mb2[j, TOP:, :].astype(F32)
+            nm = jnp.zeros((32, TOK), F32)
+            gt = jnp.zeros((32, TOK), F32)
+            for k in range(TOP):
+                hit = ids[k : k + 1, :] == here
+                nm = jnp.where(hit, 1.0, nm)
+                gt = jnp.where(hit, gts[k : k + 1, :], gt)
+            m_buf[j * 32 : (j + 1) * 32, :] = nm
+            gates[j * 32 : (j + 1) * 32, :] = gt
+        bef = dot(m_buf[...].astype(BF), earlier())
+        slots[...] = jnp.where(m_buf[...] > 0, bef, 99.0)
+        for j in range(8):
+            sl = slots[j * 32 : (j + 1) * 32, :]
+            gt = gates[j * 32 : (j + 1) * 32, :]
+            for s in range(CAP):
+                w2_buf[j, s * 32 : (s + 1) * 32, :] = jnp.where(sl == float(s), gt, 0.0).astype(BF)
+        for j in range(8):
+            got = dot(w2_buf[j], g2_buf[j])
+            for s in range(CAP):
+                f2_buf[pl.ds(s * 8 + j, 32, stride=CAP * 8), :] = got[s * 32 : (s + 1) * 32, :]
+        o2_buf[...] = f2_buf[...].astype(BF).reshape(16, ROWS * 8, UW)
+        h_in[pl.ds(2 * z + c, 1)] = o2_buf[pl.ds(2 * z + c, 1)]
+        to, fr = iota((128, 128), 0), iota((128, 128), 1)
+        q = lax.rem(to, 64)
+        want = (lax.rem(q, 16) // 2) * 16 + (to // 64) * 8 + (q // 16) * 2 + lax.rem(q, 2)
+        turn[...] = (fr == want).astype(BF)
+        order[...] = (2 * lax.rem(to, 64) + to // 64 == fr).astype(BF)
+
+    h3_cp = []
+
+    def across_send(n):
+        for _ in range(n):
+            i = len(h3_cp)
+            if i == len(zc):
+                return
+            dz, dc = ACROSS[i]
+            to = 2 * lax.rem(z + dz, NZ) + lax.rem(c + dc, 2)
+            cp = send(o2_buf.at[to], h_in.at[2 * z + c], h3_s, h3_r, at(dz=dz, dc=dc))
+            cp.start()
+            h3_cp.append(cp)
+
+    def across_done():
+        bulk(h_in, 15, h3_r)
+        for t in range(CAP):
+            tile = pl.ds(t * 16, 16)
+            both = [
+                jnp.concatenate([h_in[2 * k + h, tile, :] for k in range(NZ)], axis=0) for h in range(2)
+            ]
+            got = dot(turn[...], jnp.concatenate(both, axis=1)).astype(BF)
+            for h in range(2):
+                col = h * 1024 + RING * UW
+                r_buf[2 * t : 2 * t + 2, :, col : col + UW] = got[:, h * UW : (h + 1) * UW].reshape(2, 64, UW)
 
     def work(u, h):
         if h == 0:
@@ -222,6 +295,9 @@
         if h == 4:
             for a in range(8):
                 rows(u, a)
+            if u == 1:
+                across()
+            across_send(SPREAD[u])
 
     late = [steps[0]]
     for n, (u, h) in enumerate(steps[1:]):
@@ -237,27 +313,22 @@
             late = []
 
     own_li.wait()
-    for cp in li_cp:
-        cp.wait_recv()
+    bulk(lib, 7, li_r)
     eye = (iota((TOK, TOK), 0) == iota((TOK, TOK), 1)).astype(BF)
     for g in range(8):
         lit[:, g * TOK : (g + 1) * TOK] = dot(lib[g], eye, ((0,), (0,))).astype(BF)
 
     load_e.wait()
-    store_cp = []
-    for u in range(UNITS):
-        for a in range(7):
-            dx, dc = REL[a]
-            xs, cs = lax.rem(x + NX - dx, NX), lax.rem(c + dc, 2)
-            send(
-                o_buf.at[u, a], place(u, xs, cs), x_s.at[u, a], x_r.at[u, a], at(dx=dx, dc=dc)
-            ).wait_recv()
-        out_cp[u].wait()
+    for u in ORDER:
+        if u == RING:
+            across_done()
+        else:
+            taken(o_buf.at[u, pl.ds(0, 7)], x_r.at[u])
+            out_cp[u].wait()
         for h in range(2):
             cols = pl.ds(h * 1024 + u * UW, UW)
-            cp = pltpu.make_async_copy(r_buf.at[:, :, cols], grows.at[:, :, cols], loc.at[29 + 2 * u + h])
+            cp = pltpu.make_async_copy(r_buf.at[:, :, cols], grows.at[:, :, cols], loc.at[0])
             cp.start()
-            store_cp.append(cp)
 
         def score(r, carry, u=u):
             tot = jnp.zeros((64, 128), F32)
@@ -286,8 +357,14 @@
 
     lax.fori_loop(1, 64, sc_start, 0)
     t_in[pl.ds(idx, 1)] = s_out[pl.ds(idx, 1)]
-    for cp in swap + meta_cp + pending + li_cp:
-        cp.wait_send()
+    taken(x_buf.at[:, 0], xch_s)
+    taken(x_buf.at[pl.ds(0, RING), pl.ds(0, 14)], ring_s)
+    taken(o_buf.at[pl.ds(0, RING), pl.ds(0, 7)], x_s)
+    bulk(mb, 15, meta_s)
+    bulk(lib, 7, li_s)
+    bulk(g2_buf, 6, h_s)
+    bulk(mb2, 6, h2_s)
+    bulk(h_in, 15, h3_s)
     bulk(t_in, 63, sc_r)
 
     back = t_in[...].reshape(64, 128)
@@ -300,22 +377,17 @@
         scaled.append(v)
     scaled = jnp.concatenate(scaled, axis=0)
     logits = scaled - own_gate[...] * jnp.sum(scaled, axis=0, keepdims=True)
-    order = (2 * lax.rem(lane_row, 64) + lane_row // 64 == iota((TOK, TOK), 1)).astype(BF)
-    glt[...] = dot(logits.astype(BF), order, ((0,), (0,))).astype(BF)
-
-    gl_cp = []
+    glt[...] = dot(logits.astype(BF), order[...], ((0,), (0,))).astype(BF)
+
     for i, (dy, dc) in enumerate(yc):
-        cp = send(glt, glb.at[2 * y + c], gl_s.at[i], gl_r.at[i], at(dy=dy, dc=dc))
-        cp.start()
-        gl_cp.append(cp)
+        cp = send(glt, glb.at[2 * y + c], gl_s, gl_r, at(dy=dy, dc=dc))
+        cp.start()
     glb[pl.ds(2 * y + c, 1)] = glt[...].reshape(1, TOK, EXP)
     load_rw.wait()
     gin[...] = dot(glt[...], rw[...], ((1,), (1,))).astype(BF)
     cp = pltpu.make_async_copy(gin, gin_out, loc.at[1])
     cp.start()
-    store_cp.append(cp)
-    for cp in gl_cp:
-        cp.wait_recv()
+    bulk(glb, 7, gl_r)
     part[...] = dot(lit[...], glb[...].reshape(8 * TOK, EXP))
 
     chip = x * NZ + z
@@ -334,8 +406,7 @@
     lax.fori_loop(1, 32, rs_start, 0)
     rb[pl.ds(chip, 1)] = part[pl.ds(pl.multiple_of(chip * 8, 8), 8), :].reshape(1, 8, EXP)
     bulk(s_out, 63, sc_s)
-    for cp in gl_cp:
-        cp.wait_send()
+    bulk(glb, 7, gl_s)
     bulk(rb, 31, rs_r)
     fin[...] = jnp.sum(rb[...], axis=0)
 
@@ -350,57 +421,47 @@
     bulk(ag, 31, a1_r)
     half[...] = ag[...].reshape(256, EXP).astype(BF)
 
-    a2_cp = []
     for i in range(1, NY):
-        cp = send(half, agb.at[2 * y + c], a2_s.at[i], a2_r.at[i], at(dy=i))
-        cp.start()
-        a2_cp.append(cp)
-    a3_cp = []
-
-    def swap_part(i, g, src):
-        cp = send(src, agb.at[g], a3_s.at[i], a3_r.at[i], at(dc=1))
-        cp.start()
-        a3_cp.append(cp)
-
-    swap_part(0, 2 * y + c, half)
+        cp = send(half, agb.at[2 * y + c], a2_s, a2_r.at[i], at(dy=i))
+        cp.start()
+
+    def swap_part(g, src):
+        send(src, agb.at[g], a3_s, a3_r, at(dc=1)).start()
+
+    swap_part(2 * y + c, half)
     agb[pl.ds(2 * y + c, 1)] = half[...].reshape(1, 256, EXP)
     bulk(ag, 31, a1_s)
-    for cp in store_cp:
-        cp.wait()
+    taken(r_buf, loc.at[0])
+    taken(gin, loc.at[1])
     for i in range(1, NY):
         ys = lax.rem(y + NY - i, NY)
-        send(half, agb.at[2 * ys + c], a2_s.at[i], a2_r.at[i], at(dy=i)).wait_recv()
-        swap_part(i, 2 * ys + c, agb.at[2 * ys + c])
-    for i in range(NY):
-        ys = lax.rem(y + NY - i, NY)
-        g = 2 * ys + 1 - c
-        send(half, agb.at[g], a3_s.at[i], a3_r.at[i], at(dc=1)).wait_recv()
-
+        send(half, agb.at[2 * ys + c], a2_s, a2_r.at[i], at(dy=i)).wait_recv()
+        swap_part(2 * ys + c, agb.at[2 * ys + c])
+    bulk(agb, NY, a3_r)
     store = pltpu.make_async_copy(agb, agb_out, loc.at[0])
     store.start()
-    for cp in a2_cp + a3_cp:
-        cp.wait_send()
+    bulk(agb, NY - 1, a2_s)
+    bulk(agb, NY, a3_s)
     store.wait()
 
 
 def writer(rows_in, gin_in, agb_in, grows, gin_out, grout, rows, gin, parts, wide, loc, sto):
-    pieces = [(rows_in.at[pl.ds(3 * i, 3)], rows.at[pl.ds(3 * i, 3)], grows.at[pl.ds(3 * i, 3)]) for i in range(6)]
-    pieces.append((gin_in, gin, gin_out))
-    load = pltpu.make_async_copy(agb_in, parts, loc.at[7])
-    load.start()
-    loads = [pltpu.make_async_copy(a, b, loc.at[i]) for i, (a, b, _) in enumerate(pieces)]
-    stores = [pltpu.make_async_copy(b, c, sto.at[i]) for i, (_, b, c) in enumerate(pieces)]
+    pieces = [pl.ds(3 * i, 3) for i in range(6)]
+    loads = [pltpu.make_async_copy(agb_in, parts, loc.at[6]), pltpu.make_async_copy(gin_in, gin, loc.at[7])]
+    loads += [pltpu.make_async_copy(rows_in.at[p], rows.at[p], loc.at[i]) for i, p in enumerate(pieces)]
     for cp in loads:
         cp.start()
-    load.wait()
+    loads[0].wait()
     wide[...] = parts[...].reshape(D, EXP).astype(F32)
-    stores.append(pltpu.make_async_copy(wide, grout, sto.at[7]))
-    stores[7].start()
-    for i in range(7):
-        loads[i].wait()
-        stores[i].start()
-    for cp in stores:
-        cp.wait()
+    pltpu.make_async_copy(wide, grout, sto.at[0]).start()
+    loads[1].wait()
+    pltpu.make_async_copy(gin, gin_out, sto.at[1]).start()
+    for i, p in enumerate(pieces):
+        loads[2 + i].wait()
+        pltpu.make_async_copy(rows.at[p], grows.at[p], sto.at[2]).start()
+    pltpu.make_async_copy(wide, grout, sto.at[0]).wait()
+    pltpu.make_async_copy(gin, gin_out, sto.at[1]).wait()
+    pltpu.make_async_copy(rows, grows, sto.at[2]).wait()
 
 
 def body(grad_out, layer_input, router_weight, gate_probs, expert_ids, expert_out):
@@ -433,6 +494,14 @@
             vm((256, TOK), F32),
             vm((256, TOK), F32),
             vm((256, TOK), F32),
+            vm((8, 2 * TOP, TOK), BF),
+            vm((8, TOK, UW), BF),
+            vm((8, CAP * 32, TOK), BF),
+            vm((16 * ROWS * 8, UW), F32),
+            vm((16, ROWS * 8, UW), BF),
+            vm((16, ROWS * 8, UW), BF),
+            vm((128, 128), BF),
+            vm((128, 128), BF),
             vm((EXP, TOK), F32),
             vm((EXP, TOK), F32),
             vm((ROWS, 64, 128), F32),
@@ -447,18 +516,19 @@
             vm((8, EXP), F32),
             vm((32, 8, EXP), F32),
             vm((256, EXP), BF),
-            sem((45,)),
-            sem((UNITS,)), sem((UNITS,)),
-            sem((UNITS, 2, 4)), sem((UNITS, 2, 4)),
-            sem((15,)), sem((15,)),
-            sem((7,)), sem((7,)),
-            sem((UNITS, 7)), sem((UNITS, 7)),
-            sem, sem,
-            sem((7,)), sem((7,)),
-            sem, sem,
-            sem, sem,
-            sem((NY,)), sem((NY,)),
-            sem((NY,)), sem((NY,)),
+            sem((22,)),
+            sem, sem((UNITS,)),
+            sem, sem((RING, 2, 4)),
+            sem, sem,
+            sem, sem,
+            sem, sem((RING,)),
+            sem, sem, sem, sem, sem, sem,
+            sem, sem,
+            sem, sem,
+            sem, sem,
+            sem, sem,
+            sem, sem((NY,)),
+            sem, sem,
         ],
         compiler_params=pltpu.CompilerParams(
             collective_id=0, has_side_effects=True, vmem_limit_bytes=57 * 2**20
@@ -475,7 +545,7 @@
         out_specs=(hbm, hbm, hbm),
         scratch_shapes=[
             vm((ROWS, 64, D), BF), vm((TOK, D), BF), vm((8, 256, EXP), BF), vm((D, EXP), F32),
-            sem((8,)), sem((8,)),
+            sem((8,)), sem((3,)),
         ],
         compiler_params=pltpu.CompilerParams(vmem_limit_bytes=57 * 2**20),
     )(*results)

time: 120 us -> 114 us (0.950)
  Pallas kernels: 120 us -> 113 us
    pallas_call x1, Pallas kernels: 115 us -> 108 us  [body(): pl.pallas_call(kernel, out_shape=(jax.ShapeDtypeStruct((ROWS, 64, D), BF)...]
where the time goes in v3:
time: 114 us; the launch traced here: 113 us
  Pallas kernels  113 us (99%)
    pallas_call x1, Pallas kernels, body(): pl.pallas_call(kernel, out_shape=(jax.ShapeDtypeStruct((ROWS, 64, D), BF)...  108 us
    pallas_call x1, Pallas kernels, body(): pl.pallas_call(writer, out_shape=(jax.ShapeDtypeStruct((ROWS, 64, D), BF)...  5.1 us

profile of v3, /device:TPU:1, one launch (start us, length us, event | category | flops | bytes accessed | tf_op | source)
XLA Modules:
  0.0 113.4 jit_solution(3449060006718281521)
XLA Ops:
  0.6 107.6 %shard_map.85 = (bf16[18,64,2048]{2,1,0:T(8,128)(2,1)}, bf16[128,2048]{1,0:T(8,128)(2,1)}, bf16[8,256,128]{2,1,0:T(8,128)(2,1)}) custom-call(bf16[128,2048]{1,0:T(8,128)(2,1)} %go.1, bf16[128,2048]{1,0:T(8,128)(2,1)} %li.1, bf16[2048,128]{1,0:T(8,128)(2,1)} %rw_in.1, s32[8,128]{1,0:T(8,128)} %bitcast.13, f32[8,128]{1,0:T(8,128)} %bitcast.14, ...), custom_call_target="tpu_custom_call" | custom-call | tf_op jit(solution)/shard_map/pallas_call | solution.py:471
  108.3 5.1 %shard_map.86 = (bf16[18,64,2048]{2,1,0:T(8,128)(2,1)}, bf16[128,2048]{1,0:T(8,128)(2,1)}, f32[2048,128]{1,0:T(8,128)}) custom-call(bf16[18,64,2048]{2,1,0:T(8,128)(2,1)} %get-tuple-element.9.rows_in, bf16[128,2048]{1,0:T(8,128)(2,1)} %get-tuple-element.10.gin_in, bf16[8,256,128]{2,1,0:T(8,128)(2,1)} %get-tuple-element.11.agb_in), custom_call_target="tpu_custom_call" | custom-call | tf_op jit(solution)/shard_map/pallas_call | solution.py:537

commit v4 on v3

--- a/solution.py
+++ b/solution.py
@@ -16,7 +16,7 @@
 STEP, HOP = 4.8, 3.3
 ORDER = (0, 1, 2, 3, 4, 5, 7, 6)
 ACROSS = tuple((dz, dc) for dz in (4, 3, 5, 2, 6, 1, 7) for dc in range(2)) + ((0, 1),)
-SPREAD = (0, 0, 0, 0, 0, 5, 10)
+SPREAD = {(5, 4): 2, (6, 3): 13}
 REL = ((2, 0), (2, 1), (1, 0), (3, 0), (1, 1), (3, 1), (0, 1), (0, 0))
 
 
@@ -34,9 +34,9 @@
 
 def kernel(
     go, li, rw_in, ids_in, gates_in, eo, grows, gin_out, agb_out,
-    x_buf, f_buf, o_buf, w_buf, r_buf, gin, agb, e_buf, rw, ids_own, gates_own, meta, mb, slots, gates, m_buf, mb2, g2_buf, w2_buf, f2_buf, o2_buf, h_in, turn, order,
-    own_slot, own_gate, acc, s_out, t_in, lib, lit, glt, glb, part, rb, fin, ag, half,
-    loc, xch_s, xch_r, ring_s, ring_r, meta_s, meta_r, li_s, li_r, x_s, x_r, h_s, h_r, h2_s, h2_r, h3_s, h3_r,
+    x_buf, f_buf, o_buf, w_buf, r_buf, gin, agb, e_buf, rw, ids_own, gates_own, meta, mb, slots, gates, m_buf, mb2, g2_buf, w2_buf, f2_buf, o2_buf, h_in, turn, mb3, few, fews,
+    own_slot, own_gate, acc, s_out, t_in, count, lib, lit, glt, glb, part, rb, fin, ag, half,
+    loc, xch_s, xch_r, ring_s, ring_r, meta_s, meta_r, li_s, li_r, x_s, x_r, h_s, h_r, h2_s, h2_r, h3_s, h3_r, h4_s, h4_r,
     sc_s, sc_r, gl_s, gl_r, rs_s, rs_r, a1_s, a1_r, a2_s, a2_r, a3_s, a3_r,
 ):
     y = lax.axis_index("dp")
@@ -120,7 +120,34 @@
             at(dz=1 if d == 0 else NZ - 1),
         ).wait_recv()
 
+    def ring0(d, h, i):
+        blk = x_buf.at[0, pl.ds(2 * came(d, h - 1) + (c if i == 0 else 1 - c), 1)]
+        return send(
+            blk, blk, ring_s, ring_r.at[RING * i, d, h - 1], at(dz=1 if d == 0 else NZ - 1)
+        )
+
+    def landed0(d, h, i):
+        blk = x_buf.at[0, pl.ds(2 * came(d, h) + (c if i == 0 else 1 - c), 1)]
+        send(
+            blk, blk, ring_s, ring_r.at[RING * i, d, h - 1], at(dz=1 if d == 0 else NZ - 1)
+        ).wait_recv()
+
+    def hop0(h):
+        for i in range(2):
+            if h == 0 and i == 0:
+                own_half[0].wait()
+            if h == 0 and i == 1:
+                swap[0].wait_recv()
+            for d in range(2):
+                if 0 < h <= HOPS[0][d]:
+                    landed0(d, h, i)
+                if h < HOPS[0][d]:
+                    ring0(d, h + 1, i).start()
+
     def hop(u, h):
+        if u == 0:
+            hop0(h)
+            return
         if h == 0:
             own_half[u].wait()
             swap[u].wait_recv()
@@ -140,6 +167,9 @@
         cp.start()
     for u in range(2, RING):
         swap[u].start()
+    for dy, dc in yc:
+        send(meta, mb3.at[2 * y + c], h4_s, h4_r, at(dy=dy, dc=dc)).start()
+    mb3[pl.ds(2 * y + c, 1)] = meta[...].reshape(1, 2 * TOP, TOK)
 
     own_half[RING].wait()
     swap[RING].wait_recv()
@@ -259,7 +289,6 @@
         q = lax.rem(to, 64)
         want = (lax.rem(q, 16) // 2) * 16 + (to // 64) * 8 + (q // 16) * 2 + lax.rem(q, 2)
         turn[...] = (fr == want).astype(BF)
-        order[...] = (2 * lax.rem(to, 64) + to // 64 == fr).astype(BF)
 
     h3_cp = []
 
@@ -297,12 +326,12 @@
                 rows(u, a)
             if u == 1:
                 across()
-            across_send(SPREAD[u])
 
     late = [steps[0]]
     for n, (u, h) in enumerate(steps[1:]):
         hop(u, h)
         late.append((u, h))
+        across_send(SPREAD.get((u, h), 0))
         if n == 2:
             for cp in li_cp:
                 cp.start()
@@ -345,11 +374,11 @@
     total = jnp.zeros((64, 128), F32)
     for r in range(ROWS):
         total = jnp.where(iota((64, 128), 1) == r, jnp.sum(acc[r], axis=1, keepdims=True), total)
-    s_out[...] = total.reshape(64, 1, 128)
+    s_out[...] = total
 
     def sc(i):
         to = lax.rem(idx + i, 64)
-        return send(s_out.at[to], t_in.at[idx], sc_s, sc_r, (y, to))
+        return send(s_out.at[pl.ds(to, 1)], t_in.at[pl.ds(idx, 1)], sc_s, sc_r, (y, to))
 
     def sc_start(i, carry):
         sc(i).start()
@@ -365,9 +394,11 @@
     bulk(g2_buf, 6, h_s)
     bulk(mb2, 6, h2_s)
     bulk(h_in, 15, h3_s)
-    bulk(t_in, 63, sc_r)
-
-    back = t_in[...].reshape(64, 128)
+    bulk(mb3, 7, h4_s)
+    bulk(mb3, 7, h4_r)
+    taken(count, sc_r)
+
+    back = t_in[...]
     scaled = []
     for l in range(2):
         sl = own_slot[l * 64 : (l + 1) * 64, :]
@@ -376,50 +407,72 @@
             v = jnp.where(sl == float(s), back[:, l * CAP + s : l * CAP + s + 1], v)
         scaled.append(v)
     scaled = jnp.concatenate(scaled, axis=0)
-    logits = scaled - own_gate[...] * jnp.sum(scaled, axis=0, keepdims=True)
-    glt[...] = dot(logits.astype(BF), order[...], ((0,), (0,))).astype(BF)
-
-    for i, (dy, dc) in enumerate(yc):
-        cp = send(glt, glb.at[2 * y + c], gl_s, gl_r, at(dy=dy, dc=dc))
-        cp.start()
-    glb[pl.ds(2 * y + c, 1)] = glt[...].reshape(1, TOK, EXP)
+    total = jnp.sum(scaled, axis=0, keepdims=True)
+    for k in range(TOP):
+        mine = jnp.sum(jnp.where(ids_own[k : k + 1, :] == expert, scaled, 0.0), axis=0, keepdims=True)
+        few[k : k + 1, :] = mine - gates_own[k : k + 1, :] * total
+
+    for dy, dc in yc:
+        send(few, fews.at[2 * y + c], gl_s, gl_r, at(dy=dy, dc=dc)).start()
+    fews[pl.ds(2 * y + c, 1)] = few[...].reshape(1, TOP, TOK)
+
+    def spread(ids, vals):
+        got = jnp.zeros((EXP, TOK), F32)
+        for k in range(TOP):
+            got = jnp.where(ids[k : k + 1, :] == lane_row, vals[k : k + 1, :], got)
+        return got.astype(BF)
+
+    glt[...] = spread(ids_own[...], few[...])
     load_rw.wait()
-    gin[...] = dot(glt[...], rw[...], ((1,), (1,))).astype(BF)
-    cp = pltpu.make_async_copy(gin, gin_out, loc.at[1])
-    cp.start()
-    bulk(glb, 7, gl_r)
-    part[...] = dot(lit[...], glb[...].reshape(8 * TOK, EXP))
+    gin[...] = dot(glt[...], rw[...], ((0,), (1,))).astype(BF)
+    pltpu.make_async_copy(gin, gin_out, loc.at[1]).start()
+    bulk(fews, 7, gl_r)
+    for j in range(8):
+        glb[:, j * TOK : (j + 1) * TOK] = spread(mb3[j, 0:TOP, :].astype(F32).astype(jnp.int32), fews[j])
+    part[...] = dot(lit[...], glb[...], ((1,), (1,))).astype(BF)
 
     chip = x * NZ + z
-
-    def chip_at(i):
-        q = lax.rem(chip + i, 32)
-        return q, (y, q * 2 + c)
+    seat = x * 4 + z // 2
+    owner = lax.rem(z, 2) == 0
+
+    def seat_at(q):
+        return (y, (q // 4) * 16 + lax.rem(q, 4) * 4 + c)
 
     def rs_start(i, carry):
-        q, to = chip_at(i)
+        q = lax.rem(seat + i, 16)
         send(
-            part.at[pl.ds(pl.multiple_of(q * 8, 8), 8)], rb.at[chip], rs_s, rs_r, to
+            part.at[pl.ds(pl.multiple_of(q * 16, 16), 16)], rb.at[chip], rs_s, rs_r, seat_at(q)
         ).start()
         return carry
 
-    lax.fori_loop(1, 32, rs_start, 0)
-    rb[pl.ds(chip, 1)] = part[pl.ds(pl.multiple_of(chip * 8, 8), 8), :].reshape(1, 8, EXP)
-    bulk(s_out, 63, sc_s)
-    bulk(glb, 7, gl_s)
-    bulk(rb, 31, rs_r)
-    fin[...] = jnp.sum(rb[...], axis=0)
-
     def a1_start(i, carry):
-        q, to = chip_at(i)
-        send(fin, ag.at[chip], a1_s, a1_r, to).start()
+        q = lax.rem(chip + i, 32)
+        send(fin, ag.at[seat], a1_s, a1_r, (y, q * 2 + c)).start()
         return carry
 
-    lax.fori_loop(1, 32, a1_start, 0)
-    ag[pl.ds(chip, 1)] = fin[...].reshape(1, 8, EXP)
-    bulk(rb, 31, rs_s)
-    bulk(ag, 31, a1_r)
-    half[...] = ag[...].reshape(256, EXP).astype(BF)
+    lax.fori_loop(1, 16, rs_start, 0)
+
+    @pl.when(owner)
+    def _():
+        rb[pl.ds(chip, 1)] = part[pl.ds(pl.multiple_of(seat * 16, 16), 16), :].reshape(1, 16, EXP)
+        taken(count, sc_s)
+        bulk(fews, 7, gl_s)
+        bulk(rb, 31, rs_r)
+        fin[...] = jnp.sum(rb[...].astype(F32), axis=0).astype(BF)
+        lax.fori_loop(1, 32, a1_start, 0)
+        ag[pl.ds(seat, 1)] = fin[...].reshape(1, 16, EXP)
+        bulk(rb, 15, rs_s)
+        bulk(ag, 15, a1_r)
+
+    @pl.when(jnp.logical_not(owner))
+    def _():
+        rs_start(0, 0)
+        taken(count, sc_s)
+        bulk(fews, 7, gl_s)
+        bulk(rb, 16, rs_s)
+        bulk(ag, 16, a1_r)
+
+    half[...] = ag[...].reshape(256, EXP)
 
     for i in range(1, NY):
         cp = send(half, agb.at[2 * y + c], a2_s, a2_r.at[i], at(dy=i))
@@ -430,7 +483,11 @@
 
     swap_part(2 * y + c, half)
     agb[pl.ds(2 * y + c, 1)] = half[...].reshape(1, 256, EXP)
-    bulk(ag, 31, a1_s)
+
+    @pl.when(owner)
+    def _():
+        bulk(rb, 31, a1_s)
+
     taken(r_buf, loc.at[0])
     taken(gin, loc.at[1])
     for i in range(1, NY):
@@ -501,28 +558,31 @@
             vm((16, ROWS * 8, UW), BF),
             vm((16, ROWS * 8, UW), BF),
             vm((128, 128), BF),
-            vm((128, 128), BF),
+            vm((8, 2 * TOP, TOK), BF),
+            vm((TOP, TOK), F32),
+            vm((8, TOP, TOK), F32),
             vm((EXP, TOK), F32),
             vm((EXP, TOK), F32),
             vm((ROWS, 64, 128), F32),
-            vm((64, 1, 128), F32),
-            vm((64, 1, 128), F32),
+            vm((64, 128), F32),
+            vm((64, 128), F32),
+            vm((63, 1, 128), F32),
             vm((8, TOK, WID), BF),
             vm((WID, 8 * TOK), BF),
-            vm((TOK, EXP), BF),
-            vm((8, TOK, EXP), BF),
-            vm((WID, EXP), F32),
-            vm((32, 8, EXP), F32),
-            vm((8, EXP), F32),
-            vm((32, 8, EXP), F32),
+            vm((EXP, TOK), BF),
+            vm((EXP, 8 * TOK), BF),
+            vm((WID, EXP), BF),
+            vm((32, 16, EXP), BF),
+            vm((16, EXP), BF),
+            vm((16, 16, EXP), BF),
             vm((256, EXP), BF),
             sem((22,)),
             sem, sem((UNITS,)),
-            sem, sem((RING, 2, 4)),
+            sem, sem((RING + 1, 2, 4)),
             sem, sem,
             sem, sem,
             sem, sem((RING,)),
-            sem, sem, sem, sem, sem, sem,
+            sem, sem, sem, sem, sem, sem, sem, sem,
             sem, sem,
             sem, sem,
             sem, sem,

time: 114 us -> 108 us (0.947)
  Pallas kernels: 113 us -> 107 us
    pallas_call x1, Pallas kernels: 108 us -> 102 us  [body(): pl.pallas_call(kernel, out_shape=(jax.ShapeDtypeStruct((ROWS, 64, D), BF)...]
where the time goes in v4:
time: 108 us
  Pallas kernels  107 us (99%)
    pallas_call x1, Pallas kernels, body(): pl.pallas_call(kernel, out_shape=(jax.ShapeDtypeStruct((ROWS, 64, D), BF)...  102 us
    pallas_call x1, Pallas kernels, body(): pl.pallas_call(writer, out_shape=(jax.ShapeDtypeStruct((ROWS, 64, D), BF)...  5.1 us

profile of v4, /device:TPU:1, one launch (start us, length us, event | category | flops | bytes accessed | tf_op | source)
XLA Modules:
  0.0 108.1 jit_solution(11169404825657242286)
XLA Ops:
  0.6 102.3 %shard_map.85 = (bf16[18,64,2048]{2,1,0:T(8,128)(2,1)}, bf16[128,2048]{1,0:T(8,128)(2,1)}, bf16[8,256,128]{2,1,0:T(8,128)(2,1)}) custom-call(bf16[128,2048]{1,0:T(8,128)(2,1)} %go.1, bf16[128,2048]{1,0:T(8,128)(2,1)} %li.1, bf16[2048,128]{1,0:T(8,128)(2,1)} %rw_in.1, s32[8,128]{1,0:T(8,128)} %bitcast.13, f32[8,128]{1,0:T(8,128)} %bitcast.14, ...), custom_call_target="tpu_custom_call" | custom-call | tf_op jit(solution)/shard_map/pallas_call | solution.py:528
  103.0 5.1 %shard_map.86 = (bf16[18,64,2048]{2,1,0:T(8,128)(2,1)}, bf16[128,2048]{1,0:T(8,128)(2,1)}, f32[2048,128]{1,0:T(8,128)}) custom-call(bf16[18,64,2048]{2,1,0:T(8,128)(2,1)} %get-tuple-element.9.rows_in, bf16[128,2048]{1,0:T(8,128)(2,1)} %get-tuple-element.10.gin_in, bf16[8,256,128]{2,1,0:T(8,128)(2,1)} %get-tuple-element.11.agb_in), custom_call_target="tpu_custom_call" | custom-call | tf_op jit(solution)/shard_map/pallas_call | solution.py:597

commit v5 on v4

--- a/solution.py
+++ b/solution.py
@@ -139,9 +139,9 @@
             if h == 0 and i == 1:
                 swap[0].wait_recv()
             for d in range(2):
-                if 0 < h <= HOPS[0][d]:
+                if 0 < h < 4 or h == 4 and d == i:
                     landed0(d, h, i)
-                if h < HOPS[0][d]:
+                if h < 3 or h == 3 and d == i:
                     ring0(d, h + 1, i).start()
 
     def hop(u, h):

time: 108 us -> 107 us (level)
    pallas_call x1, Pallas kernels: 102 us -> 101 us  [body(): pl.pallas_call(kernel, out_shape=(jax.ShapeDtypeStruct((ROWS, 64, D), BF)...]
where the time goes in v5:
time: 107 us
  Pallas kernels  106 us (99%)
    pallas_call x1, Pallas kernels, body(): pl.pallas_call(kernel, out_shape=(jax.ShapeDtypeStruct((ROWS, 64, D), BF)...  101 us
    pallas_call x1, Pallas kernels, body(): pl.pallas_call(writer, out_shape=(jax.ShapeDtypeStruct((ROWS, 64, D), BF)...  5.1 us

profile of v5, /device:TPU:1, one launch (start us, length us, event | category | flops | bytes accessed | tf_op | source)
XLA Modules:
  0.0 107.0 jit_solution(3219177612999141184)
XLA Ops:
  0.6 101.3 %shard_map.85 = (bf16[18,64,2048]{2,1,0:T(8,128)(2,1)}, bf16[128,2048]{1,0:T(8,128)(2,1)}, bf16[8,256,128]{2,1,0:T(8,128)(2,1)}) custom-call(bf16[128,2048]{1,0:T(8,128)(2,1)} %go.1, bf16[128,2048]{1,0:T(8,128)(2,1)} %li.1, bf16[2048,128]{1,0:T(8,128)(2,1)} %rw_in.1, s32[8,128]{1,0:T(8,128)} %bitcast.13, f32[8,128]{1,0:T(8,128)} %bitcast.14, ...), custom_call_target="tpu_custom_call" | custom-call | tf_op jit(solution)/shard_map/pallas_call | solution.py:528
  101.9 5.1 %shard_map.86 = (bf16[18,64,2048]{2,1,0:T(8,128)(2,1)}, bf16[128,2048]{1,0:T(8,128)(2,1)}, f32[2048,128]{1,0:T(8,128)}) custom-call(bf16[18,64,2048]{2,1,0:T(8,128)(2,1)} %get-tuple-element.9.rows_in, bf16[128,2048]{1,0:T(8,128)(2,1)} %get-tuple-element.10.gin_in, bf16[8,256,128]{2,1,0:T(8,128)(2,1)} %get-tuple-element.11.agb_in), custom_call_target="tpu_custom_call" | custom-call | tf_op jit(solution)/shard_map/pallas_call | solution.py:597

commit v6 on v5

--- a/solution.py
+++ b/solution.py
@@ -384,7 +384,8 @@
         sc(i).start()
         return carry
 
-    lax.fori_loop(1, 64, sc_start, 0)
+    for i in range(1, 64):
+        sc_start(i, 0)
     t_in[pl.ds(idx, 1)] = s_out[pl.ds(idx, 1)]
     taken(x_buf.at[:, 0], xch_s)
     taken(x_buf.at[pl.ds(0, RING), pl.ds(0, 14)], ring_s)
@@ -450,7 +451,8 @@
         send(fin, ag.at[seat], a1_s, a1_r, (y, q * 2 + c)).start()
         return carry
 
-    lax.fori_loop(1, 16, rs_start, 0)
+    for i in range(1, 16):
+        rs_start(i, 0)
 
     @pl.when(owner)
     def _():
@@ -459,7 +461,8 @@
         bulk(fews, 7, gl_s)
         bulk(rb, 31, rs_r)
         fin[...] = jnp.sum(rb[...].astype(F32), axis=0).astype(BF)
-        lax.fori_loop(1, 32, a1_start, 0)
+        for i in range(1, 32):
+            a1_start(i, 0)
         ag[pl.ds(seat, 1)] = fin[...].reshape(1, 16, EXP)
         bulk(rb, 15, rs_s)
         bulk(ag, 15, a1_r)

time: 107 us -> 107 us (level)
  no operation moved by 1% of the time
where the time goes in v6:
time: 107 us
  Pallas kernels  106 us (99%)
    pallas_call x1, Pallas kernels, body(): pl.pallas_call(kernel, out_shape=(jax.ShapeDtypeStruct((ROWS, 64, D), BF)...  101 us
    pallas_call x1, Pallas kernels, body(): pl.pallas_call(writer, out_shape=(jax.ShapeDtypeStruct((ROWS, 64, D), BF)...  5.1 us

profile of v6, /device:TPU:1, one launch (start us, length us, event | category | flops | bytes accessed | tf_op | source)
XLA Modules:
  0.0 106.7 jit_solution(2309086868135538230)
XLA Ops:
  0.6 101.0 %shard_map.85 = (bf16[18,64,2048]{2,1,0:T(8,128)(2,1)}, bf16[128,2048]{1,0:T(8,128)(2,1)}, bf16[8,256,128]{2,1,0:T(8,128)(2,1)}) custom-call(bf16[128,2048]{1,0:T(8,128)(2,1)} %go.1, bf16[128,2048]{1,0:T(8,128)(2,1)} %li.1, bf16[2048,128]{1,0:T(8,128)(2,1)} %rw_in.1, s32[8,128]{1,0:T(8,128)} %bitcast.13, f32[8,128]{1,0:T(8,128)} %bitcast.14, ...), custom_call_target="tpu_custom_call" | custom-call | tf_op jit(solution)/shard_map/pallas_call | solution.py:531
  101.6 5.1 %shard_map.86 = (bf16[18,64,2048]{2,1,0:T(8,128)(2,1)}, bf16[128,2048]{1,0:T(8,128)(2,1)}, f32[2048,128]{1,0:T(8,128)}) custom-call(bf16[18,64,2048]{2,1,0:T(8,128)(2,1)} %get-tuple-element.9.rows_in, bf16[128,2048]{1,0:T(8,128)(2,1)} %get-tuple-element.10.gin_in, bf16[8,256,128]{2,1,0:T(8,128)(2,1)} %get-tuple-element.11.agb_in), custom_call_target="tpu_custom_call" | custom-call | tf_op jit(solution)/shard_map/pallas_call | solution.py:600
